TPU v7x, 512 devices: a whole 4x8x8 slice. The times are simulated.
512 devices in a mesh: dp: 16 (over y, core), code: 32 (over x, z).
Axes of the slice: x: 4, y: 8, z: 8, core: 2. Of those that a mesh axis runs over, the one named last changes fastest.
Arguments:
- latents: bfloat16 [8192, 256], P('dp')
- upstream: bfloat16 [8192, 256], P('dp'), may hold values from -6 to 6
- targets: int32 [8192], P('dp'), may hold values from 0 to 131071
- codebook: bfloat16 [131072, 256], P('code')
Outputs:
- latent_grad: float32 [8192, 256], P('dp')
- codebook_grad: float32 [131072, 256], P(('code', 'dp'))
All inputs are finite; a program needn't handle non-finite values.
Results may differ from a plain program's by a relative error of at most 0.0013.
Values sent between devices are 32-bit elements; how exact they have to be, the bound alone decides.
No kernel may reach another device: no remote copies, remote signals or barrier semaphores. Data moves between devices by JAX's collectives and lax.ppermute only.
A program may use at most 64 MiB of HBM per device.

v0:
```python
import jax
import jax.numpy as jnp
from jax import lax
from jax.sharding import PartitionSpec as P


def shards(latents, upstream, targets, codebook):
    rows = latents.shape[0]
    local_codes = codebook.shape[0]
    contract = (((1,), (1,)), ((), ()))
    scores = lax.dot_general(latents, codebook, contract, preferred_element_type=jnp.float32)
    dprob = lax.dot_general(upstream, codebook, contract, preferred_element_type=jnp.float32)
    local_top = jnp.max(scores, axis=1)
    top = lax.pmax(local_top, "code")
    expo = jnp.exp(scores - top[:, None])
    total, weighted = lax.psum((jnp.sum(expo, axis=1), jnp.sum(expo * dprob, axis=1)), "code")
    probs = expo / total[:, None]
    rowdot = weighted / total
    local_target = targets - lax.axis_index("code") * local_codes
    columns = lax.broadcasted_iota(jnp.int32, (rows, local_codes), 1)
    soft_part = probs * (dprob - rowdot[:, None]) + probs
    dscore = jnp.where(columns == local_target[:, None], soft_part - 1.0, soft_part).astype(
        jnp.bfloat16
    )
    probs_low = probs.astype(jnp.bfloat16)
    lat_part = jnp.dot(dscore, codebook, preferred_element_type=jnp.float32)
    latent_grad = lax.psum(lat_part, "code")
    left = jnp.concatenate([dscore, probs_low], axis=0)
    stacked = jnp.concatenate([latents, upstream], axis=0)
    term = lax.dot_general(
        left, stacked, (((0,), (0,)), ((), ())), preferred_element_type=jnp.float32
    )
    codebook_grad = lax.psum_scatter(term, "dp", scatter_dimension=0, tiled=True)
    return (latent_grad, codebook_grad)


def solution(mesh):
    return jax.shard_map(
        shards,
        mesh=mesh,
        in_specs=(P("dp", None), P("dp", None), P("dp"), P("code", None)),
        out_specs=(P("dp", None), P(("code", "dp"), None)),
        check_vma=False,
    )
```

profile of v0, /device:TPU:1, one launch (start us, length us, event | category | flops | bytes accessed | tf_op | source)
XLA Modules:
  0.0 345.5 jit_solution(17750143615457018137)
XLA Ops:
  8.0 0.0 copy-start
  8.0 0.0 copy-start.4
  8.0 0.0 copy-start.2
  8.0 0.0 all-reduce.3.cloned.1.call-start
  8.1 1.5 copy-done
  9.6 5.5 %fusion.12 = (f32[512]{0:T(512)S(1)}, f32[512,4096]{1,0:T(8,128)}) fusion(bf16[512,256]{1,0:T(8,128)(2,1)} %param.4, bf16[4096,256]{1,0:T(8,128)(2,1)S(1)} %copy-done), kind=kOutput, calls=%fused_computation.18 | convolution fusion | flops 1075838464 | bytes 10749952 | tf_op jit(solution)/shard_map/dot_general | solution.py:11
  15.1 67.8 %pmax.7 = f32[512]{0:T(512)S(1)} all-reduce(f32[512]{0:T(512)S(1)} %get-tuple-element.8), channel_id=1, replica_groups=mesh['dp'=16,'code'=32] {'code'}, use_global_device_ids=true, to_apply=%region_1.0 | all-reduce | flops 512 | bytes 4096 | tf_op jit(solution)/shard_map/pmax | solution.py:14
  82.8 0.0 copy-done.4
  82.8 0.0 copy-done.2
  82.8 6.5 %fusion.6 = (f32[512]{0:T(512)S(1)}, f32[512]{0:T(512)S(1)}, f32[512,4096]{1,0:T(8,128)}) fusion(f32[512,4096]{1,0:T(8,128)} %get-tuple-element.9, f32[512]{0:T(512)S(1)} %pmax.7, bf16[512,256]{1,0:T(8,128)(2,1)S(1)} %copy-done.2, bf16[4096,256]{1,0:T(8,128)(2,1)S(1)} %copy-done), kind=kOutput, calls=%fused_computation.11 | convolution fusion | flops 1082129408 | bytes 19142656 | tf_op jit(solution)/shard_map/dot_general | solution.py:12
  89.4 55.8 %all-reduce = (f32[512]{0:T(512)S(1)}, f32[512]{0:T(512)S(1)}) all-reduce(f32[512]{0:T(512)S(1)} %get-tuple-element.3, f32[512]{0:T(512)S(1)} %get-tuple-element.2), channel_id=1, replica_groups=mesh['dp'=16,'code'=32] {'code'}, use_global_device_ids=true, to_apply=%region_5.0 | all-reduce | flops 1024 | bytes 8192 | tf_op jit(solution)/shard_map/psum | solution.py:16
  145.1 0.0 copy-start.3
  145.2 9.3 %fusion.11 = (bf16[512,4096]{1,0:T(8,128)(2,1)}, bf16[512,4096]{1,0:T(8,128)(2,1)S(1)}) fusion(f32[512]{0:T(512)S(1)} %get-tuple-element.5, f32[512,4096]{1,0:T(8,128)} %get-tuple-element.9, f32[512]{0:T(512)S(1)} %pmax.7, f32[512,4096]{1,0:T(8,128)} %get-tuple-element.10, f32[512]{0:T(512)S(1)} %div.13, s32[512]{0:T(512)S(1)} %broadcast_subtract_fusion), kind=kLoop, calls=%fused_computation.17 | loop fusion | flops 20971520 | bytes 25174016 | tf_op jit(solution)/shard_map/convert_element_type | solution.py:25
  154.4 0.0 copy-start.1
  154.4 1.9 copy-done.1
  156.3 2.0 fusion.13
  158.4 0.0 all-reduce.3.cloned.1.call-update
  158.4 0.0 reduce-scatter.2.cloned.1.call-start
  158.4 0.0 copy-done.3
  158.5 7.9 %fusion.1 = f32[4096,256]{1,0:T(8,128)} fusion(bf16[512,4096]{1,0:T(8,128)(2,1)} %get-tuple-element.6, bf16[512,4096]{1,0:T(8,128)(2,1)} %copy-done.1, bf16[512,256]{1,0:T(8,128)(2,1)S(1)} %copy-done.2, bf16[512,256]{1,0:T(8,128)(2,1)S(1)} %copy-done.3), kind=kOutput, calls=%fused_computation.3 | convolution fusion | flops 2165309440 | bytes 13107200 | tf_op jit(solution)/shard_map/dot_general | solution.py:30
  166.4 0.0 reduce-scatter.2.cloned.1.call-update
  166.4 169.8 %all-reduce.3.cloned.1.call-done = f32[512,256]{1,0:T(8,128)} async-done(((f32[512,256]{1,0:T(8,128)}), f32[512,256]{1,0:T(8,128)}) %all-reduce.3.cloned.1.call-update) | async-done | bytes 524304 | tf_op jit(solution)/shard_map/psum | solution.py:27
  336.2 0.0 reduce-scatter.2.cloned.1.call-done
  336.2 1.9 copy.7
  (2 shorter events, 0.0 us)
Async XLA Ops:
  8.0 1.6 copy-start
  8.0 74.8 %copy-start.4 = (s32[512]{0:T(512)S(1)}, s32[512]{0:T(512)}, u32[]{:S(2)}) copy-start(s32[512]{0:T(512)} %param.6) | copy-start | bytes 6148
  8.0 74.8 %copy-start.2 = (bf16[512,256]{1,0:T(8,128)(2,1)S(1)}, bf16[512,256]{1,0:T(8,128)(2,1)}, u32[]{:S(2)}) copy-start(bf16[512,256]{1,0:T(8,128)(2,1)} %param.5) | copy-start | bytes 786436
  8.0 328.1 %all-reduce.3.cloned.1.call-start = ((), (), s32[]{:S(2)}) async-start(), calls=%async_computation.1 | async-start | bytes 1048576 | tf_op jit(solution)/shard_map/psum | solution.py:27
  145.1 13.3 %copy-start.3 = (bf16[512,256]{1,0:T(8,128)(2,1)S(1)}, bf16[512,256]{1,0:T(8,128)(2,1)}, u32[]{:S(2)}) copy-start(bf16[512,256]{1,0:T(8,128)(2,1)} %param.4) | copy-start | bytes 786436
  154.4 1.9 copy-start.1
  158.4 177.8 %reduce-scatter.2.cloned.1.call-start = ((), (), s32[]{:S(2)}) async-start(), calls=%async_computation.2 | async-start | bytes 4456448 | tf_op jit(solution)/shard_map/reduce_scatter | solution.py:33
Sparse Core Ops, SparseCore 0:
  158.5 177.5 all-reduce.2
Sparse Core Ops, SparseCore 1:
  166.5 86.0 reduce-scatter.1
where the time goes:
time: 349 us; the launch traced here: 345 us
  waiting for transfers between devices  170 us (49%)
  blocking collectives  124 us (36%)
  matrix products  21.9 us (6%)
  between operations  15.5 us (4%)
  other arithmetic  9.26 us (3%)
  local copies, waits for them, and re-layouts  5.32 us (2%)
    psum x1, waiting for transfers between devices, shards(): latent_grad = lax.psum(lat_part, 'code')  170 us
    pmax x1, blocking collectives, shards(): top = lax.pmax(local_top, 'code')  67.8 us
    psum x1, blocking collectives, shards(): lax.psum((jnp.sum(expo, axis=1), jnp.sum(expo * dprob, axis=1)), 'code')  55.8 us
    convert_element_type x1, other arithmetic, shards(): probs_low = probs.astype(jnp.bfloat16)  9.25 us
    dot_general x1, matrix products, shards(): lax.dot_general(left, stacked, (((0,), (0,)), ((), ())), preferred_elemen...  7.89 us
  transfers between devices with their start and end apart: 2, of which 1 were waited for; matrix products, arithmetic and copies ran while one was open for 2% of the time, Pallas kernels for 0%

commit v1 on v0

v1 whole, which is shorter than its diff:
```python
import jax
import jax.numpy as jnp
from jax import lax
from jax.sharding import PartitionSpec as P


def shards(latents, upstream, targets, codebook):
    rows, width = latents.shape
    local_codes = codebook.shape[0]
    n_code = lax.axis_size("code")
    n_dp = lax.axis_size("dp")
    contract = (((1,), (1,)), ((), ()))
    scores = lax.dot_general(latents, codebook, contract, preferred_element_type=jnp.float32)
    dprob = lax.dot_general(upstream, codebook, contract, preferred_element_type=jnp.float32)
    top = jnp.max(scores, axis=1)
    expo = jnp.exp(scores - top[:, None])
    stats = jnp.stack([top, jnp.sum(expo, axis=1), jnp.sum(expo * dprob, axis=1)])
    every = lax.all_to_all(
        jnp.broadcast_to(stats[None], (n_code,) + stats.shape), "code", 0, 0
    )
    tops = every[:, 0]
    share = jnp.exp(tops - jnp.max(tops, axis=0)[None])
    total = jnp.sum(share * every[:, 1], axis=0)
    rowdot = jnp.sum(share * every[:, 2], axis=0) / total
    scale = jnp.exp(top - jnp.max(tops, axis=0)) / total
    probs = expo * scale[:, None]
    local_target = targets - lax.axis_index("code") * local_codes
    columns = lax.broadcasted_iota(jnp.int32, (rows, local_codes), 1)
    soft_part = probs * (dprob - rowdot[:, None]) + probs
    dscore = jnp.where(columns == local_target[:, None], soft_part - 1.0, soft_part).astype(
        jnp.bfloat16
    )
    probs_low = probs.astype(jnp.bfloat16)
    left = jnp.concatenate([dscore, probs_low], axis=0)
    stacked = jnp.concatenate([latents, upstream], axis=0)
    term = lax.dot_general(
        left, stacked, (((0,), (0,)), ((), ())), preferred_element_type=jnp.float32
    )
    chips = n_dp // 2
    term = term.reshape(chips, 2, local_codes // n_dp, width)
    core = lax.rem(lax.axis_index("dp"), 2)
    mine = lax.dynamic_index_in_dim(term, core, 1, keepdims=False)
    other = lax.dynamic_index_in_dim(term, 1 - core, 1, keepdims=False)
    got = lax.ppermute(other, "dp", [(i, i ^ 1) for i in range(n_dp)])
    half = (mine + got).reshape(local_codes // 2, width)
    groups = [[2 * y + c for y in range(chips)] for c in range(2)]
    codebook_grad = lax.psum_scatter(
        half, "dp", scatter_dimension=0, axis_index_groups=groups, tiled=True
    )
    lat_part = jnp.dot(dscore, codebook, preferred_element_type=jnp.float32)
    pieces = lax.all_to_all(
        lat_part.reshape(n_code, rows // n_code, width), "code", 0, 0
    )
    piece = jnp.sum(pieces, axis=0)
    latent_grad = lax.all_to_all(
        jnp.broadcast_to(piece[None], (n_code,) + piece.shape), "code", 0, 0
    ).reshape(rows, width)
    return (latent_grad, codebook_grad)


def solution(mesh):
    return jax.shard_map(
        shards,
        mesh=mesh,
        in_specs=(P("dp", None), P("dp", None), P("dp"), P("code", None)),
        out_specs=(P("dp", None), P(("code", "dp"), None)),
        check_vma=False,
    )
```

time: 349 us -> 123 us (0.35)
  the two profiles are of different devices: /device:TPU:1 before, /device:TPU:56 now
where the time goes in v1:
time: 123 us
  blocking collectives  43.7 us (36%)
  waiting for transfers between devices  16.9 us (14%)
  starting transfers between devices  15.1 us (12%)
  between operations  14.2 us (12%)
  matrix products  13.5 us (11%)
  other arithmetic  12 us (10%)
  local copies, waits for them, and re-layouts  7.13 us (6%)
    all_to_all x1, blocking collectives, shards(): lax.all_to_all(jnp.broadcast_to(piece[None], (n_code,) + piece.shape), 'c...  22.5 us
    all_to_all x1, blocking collectives, shards(): lax.all_to_all(lat_part.reshape(n_code, rows // n_code, width), 'code', 0...  21.2 us
    all_to_all x1, starting transfers between devices, shards(): lax.all_to_all(jnp.broadcast_to(stats[None], (n_code,) + stats.shape), 'c...  13.2 us
    all_to_all x1, waiting for transfers between devices, shards(): lax.all_to_all(jnp.broadcast_to(stats[None], (n_code,) + stats.shape), 'c...  12.4 us
    convert_element_type x1, other arithmetic, shards(): probs_low = probs.astype(jnp.bfloat16)  7.97 us
    dot_general x1, matrix products, shards(): lax.dot_general(upstream, codebook, contract, preferred_element_type=jnp....  5.16 us
    unnamed x15, local copies, waits for them, and re-layouts  4.91 us
    ppermute x1, waiting for transfers between devices, shards(): got = lax.ppermute(other, 'dp', [(i, i ^ 1) for i in range(n_dp)])  4.46 us
  transfers between devices with their start and end apart: 3, of which 2 were waited for; matrix products, arithmetic and copies ran while one was open for 3% of the time, Pallas kernels for 0%

profile of v1, /device:TPU:56, one launch (start us, length us, event | category | flops | bytes accessed | tf_op | source)
XLA Modules:
  0.0 122.5 jit_solution(17014976686134916988)
XLA Ops:
  7.2 0.0 copy-start
  7.2 0.0 copy-start.4
  7.2 1.6 %copy-done = bf16[4096,256]{1,0:T(8,128)(2,1)S(1)} copy-done((bf16[4096,256]{1,0:T(8,128)(2,1)S(1)}, bf16[4096,256]{1,0:T(8,128)(2,1)}, u32[]{:S(2)}) %copy-start) | copy-done | bytes 2097176
  8.8 2.3 %fusion.16 = (f32[512]{0:T(512)S(1)}, f32[512,4096]{1,0:T(8,128)S(1)}) fusion(bf16[512,256]{1,0:T(8,128)(2,1)} %param.4, bf16[4096,256]{1,0:T(8,128)(2,1)S(1)} %copy-done), kind=kOutput, calls=%fused_computation.31 | convolution fusion | flops 1075838464 | bytes 10749952 | tf_op jit(solution)/shard_map/dot_general | solution.py:13
  11.1 0.0 copy-start.1
  11.1 0.0 copy-done.4
  11.1 0.0 copy-start.6
  11.1 5.2 %fusion.5 = (f32[512]{0:T(512)S(1)}, f32[512]{0:T(512)S(1)}, f32[512,4096]{1,0:T(8,128)}) fusion(f32[512,4096]{1,0:T(8,128)S(1)} %get-tuple-element.15, f32[512]{0:T(512)S(1)} %get-tuple-element.14, bf16[512,256]{1,0:T(8,128)(2,1)S(1)} %copy-done.4, bf16[4096,256]{1,0:T(8,128)(2,1)S(1)} %copy-done), kind=kOutput, calls=%fused_computation.11 | convolution fusion | flops 1082129408 | bytes 19142656 | tf_op jit(solution)/shard_map/dot_general | solution.py:14
  16.3 0.6 copy-done.1
  16.8 0.7 broadcast_in_dim.4
  17.6 13.2 %all-to-all-start = ((f32[32,3,512]{2,1,0:T(4,128)}), f32[32,3,512]{2,1,0:T(4,128)S(1)}, u32[]{:S(2)}, u32[]{:S(2)}) async-start(f32[32,3,512]{2,1,0:T(4,128)} %broadcast_in_dim.4), calls=%async_computation | async-start | bytes 524288 | tf_op jit(solution)/shard_map/all_to_all | solution.py:18
  30.7 0.0 reduce-scatter.2.cloned.1.call-start
  30.8 0.0 copy-done.6
  30.8 12.4 %all-to-all-done = f32[32,3,512]{2,1,0:T(4,128)S(1)} async-done(((f32[32,3,512]{2,1,0:T(4,128)}), f32[32,3,512]{2,1,0:T(4,128)S(1)}, u32[]{:S(2)}, u32[]{:S(2)}) %all-to-all-start) | async-done | bytes 196640 | tf_op jit(solution)/shard_map/all_to_all | solution.py:18
  43.2 0.2 fusion.15
  43.4 0.0 copy-start.5
  43.5 8.0 %multiply_convert_fusion = (bf16[512,4096]{1,0:T(8,128)(2,1)S(1)}, bf16[512,4096]{1,0:T(8,128)(2,1)S(1)}) fusion(f32[512,4096]{1,0:T(8,128)} %copy-done.1, f32[512]{0:T(512)S(1)} %get-tuple-element.12, f32[512]{0:T(512)S(1)} %get-tuple-element.14, f32[512,4096]{1,0:T(8,128)} %get-tuple-element.16, f32[512]{0:T(512)S(1)} %get-tuple-element.13, ...), kind=kLoop, calls=%fused_computation.10 | loop fusion | flops 20971520 | bytes 25174016 | tf_op jit(solution)/shard_map/convert_element_type | solution.py:33
  51.4 0.0 copy-start.3
  51.4 0.0 copy-done.5
  51.5 2.6 %fusion.1 = f32[4096,256]{1,0:T(8,128)S(1)} fusion(bf16[512,4096]{1,0:T(8,128)(2,1)S(1)} %get-tuple-element.6, bf16[512,4096]{1,0:T(8,128)(2,1)S(1)} %get-tuple-element.7, bf16[512,256]{1,0:T(8,128)(2,1)S(1)} %copy-done.4, bf16[512,256]{1,0:T(8,128)(2,1)S(1)} %copy-done.5), kind=kOutput, calls=%fused_computation.3 | convolution fusion | flops 2165309440 | bytes 13107200 | tf_op jit(solution)/shard_map/dot_general | solution.py:36
  54.0 0.0 copy-done.3
  54.0 0.0 copy-start.2
  54.1 2.0 %copy-done.2 = f32[4096,256]{1,0:T(8,128)} copy-done((f32[4096,256]{1,0:T(8,128)}, f32[4096,256]{1,0:T(8,128)S(1)}, u32[]{:S(2)}) %copy-start.2) | copy-done | bytes 4194328
  56.0 1.4 %dynamic-slice_bitcast_fusion = f32[8,256,256]{2,1,0:T(8,128)} fusion(f32[8,2,256,256]{3,2,1,0:T(8,128)S(1)} %bitcast.38, s32[]{:T(128)S(6)} %select_n.13), kind=kLoop, calls=%fused_computation.13 | loop fusion | bytes 4194308 | tf_op jit(solution)/shard_map/jit(dynamic_index_in_dim)/squeeze | solution.py:43
  57.4 1.9 %collective-permute-start = (f32[8,256,256]{2,1,0:T(8,128)}, f32[8,256,256]{2,1,0:T(8,128)}, u32[]{:S(2)}, u32[]{:S(2)}) collective-permute-start(f32[8,256,256]{2,1,0:T(8,128)} %dynamic-slice_bitcast_fusion), channel_id=1, source_target_pairs={{0,32},{32,0},{64,96},{96,64},{128,160},{160,128},{192,224},{224,1... | collective-permute-start | bytes 6291464 | tf_op jit(solution)/shard_map/ppermute | solution.py:44
  59.4 4.5 %collective-permute-done = f32[8,256,256]{2,1,0:T(8,128)} collective-permute-done((f32[8,256,256]{2,1,0:T(8,128)}, f32[8,256,256]{2,1,0:T(8,128)}, u32[]{:S(2)}, u32[]{:S(2)}) %collective-permute-start) | collective-permute-done | bytes 2097184 | tf_op jit(solution)/shard_map/ppermute | solution.py:44
  63.8 3.8 %bitcast_add_fusion = f32[8,256,256]{2,1,0:T(8,128)} fusion(f32[8,256,256]{2,1,0:T(8,128)} %collective-permute-done, f32[8,2,256,256]{3,2,1,0:T(8,128)} %bitcast.39, s32[]{:T(128)S(6)} %select_n.12), kind=kLoop, calls=%fused_computation.12 | loop fusion | flops 524288 | bytes 6291460 | tf_op jit(solution)/shard_map/add | solution.py:45
  67.6 0.0 reduce-scatter.2.cloned.1.call-update
  67.6 3.4 %fusion.17 = f32[512,256]{1,0:T(8,128)S(1)} fusion(bf16[512,4096]{1,0:T(8,128)(2,1)} %copy-done.3, bf16[4096,256]{1,0:T(8,128)(2,1)S(1)} %copy-done), kind=kOutput, calls=%fused_computation.32 | convolution fusion | flops 1073741824 | bytes 6815744 | tf_op jit(solution)/shard_map/dot_general | solution.py:50
  71.1 21.2 %all_to_all.15 = f32[32,16,256]{2,1,0:T(8,128)S(1)} all-to-all(f32[32,16,256]{2,1,0:T(8,128)S(1)} %bitcast.41), channel_id=1, replica_groups=mesh['dp'=16,'code'=32] {'code'}, dimensions={0} | all-to-all | bytes 1048576 | tf_op jit(solution)/shard_map/all_to_all | solution.py:51
  92.4 0.1 broadcast_in_dim.5
  92.4 22.5 %all_to_all.16 = f32[32,16,256]{2,1,0:T(8,128)S(1)} all-to-all(f32[32,16,256]{2,1,0:T(8,128)S(1)} %broadcast_in_dim.5), channel_id=1, replica_groups=mesh['dp'=16,'code'=32] {'code'}, dimensions={0} | all-to-all | bytes 1048576 | tf_op jit(solution)/shard_map/all_to_all | solution.py:55
  114.9 0.0 reduce-scatter.2.cloned.1.call-done
  114.9 0.8 copy.30
  (5 shorter events, 0.1 us)
Async XLA Ops:
  7.2 1.6 %copy-start = (bf16[4096,256]{1,0:T(8,128)(2,1)S(1)}, bf16[4096,256]{1,0:T(8,128)(2,1)}, u32[]{:S(2)}) copy-start(bf16[4096,256]{1,0:T(8,128)(2,1)} %param.7) | copy-start | bytes 6291460
  7.2 3.9 %copy-start.4 = (bf16[512,256]{1,0:T(8,128)(2,1)S(1)}, bf16[512,256]{1,0:T(8,128)(2,1)}, u32[]{:S(2)}) copy-start(bf16[512,256]{1,0:T(8,128)(2,1)} %param.5) | copy-start | bytes 786436
  11.1 5.7 %copy-start.1 = (f32[512,4096]{1,0:T(8,128)}, f32[512,4096]{1,0:T(8,128)S(1)}, u32[]{:S(2)}) copy-start(f32[512,4096]{1,0:T(8,128)S(1)} %get-tuple-element.15) | copy-start | bytes 25165828
  11.1 19.7 %copy-start.6 = (s32[512]{0:T(512)S(1)}, s32[512]{0:T(512)}, u32[]{:S(2)}) copy-start(s32[512]{0:T(512)} %param.6) | copy-start | bytes 6148
  17.6 25.6 %all-to-all-start = ((f32[32,3,512]{2,1,0:T(4,128)}), f32[32,3,512]{2,1,0:T(4,128)S(1)}, u32[]{:S(2)}, u32[]{:S(2)}) async-start(f32[32,3,512]{2,1,0:T(4,128)} %broadcast_in_dim.4), calls=%async_computation | async-start | bytes 524288 | tf_op jit(solution)/shard_map/all_to_all | solution.py:18
  30.7 84.1 %reduce-scatter.2.cloned.1.call-start = ((), (), s32[]{:S(2)}) async-start(), calls=%async_computation.4 | async-start | bytes 2359296 | tf_op jit(solution)/shard_map/reduce_scatter | solution.py:47
  43.4 8.0 %copy-start.5 = (bf16[512,256]{1,0:T(8,128)(2,1)S(1)}, bf16[512,256]{1,0:T(8,128)(2,1)}, u32[]{:S(2)}) copy-start(bf16[512,256]{1,0:T(8,128)(2,1)} %param.4) | copy-start | bytes 786436
  51.4 2.6 %copy-start.3 = (bf16[512,4096]{1,0:T(8,128)(2,1)}, bf16[512,4096]{1,0:T(8,128)(2,1)S(1)}, u32[]{:S(2)}) copy-start(bf16[512,4096]{1,0:T(8,128)(2,1)S(1)} %get-tuple-element.7) | copy-start | bytes 12582916
  54.0 2.0 %copy-start.2 = (f32[4096,256]{1,0:T(8,128)}, f32[4096,256]{1,0:T(8,128)S(1)}, u32[]{:S(2)}) copy-start(f32[4096,256]{1,0:T(8,128)S(1)} %fusion.1) | copy-start | bytes 12582916
  57.4 6.4 %collective-permute-start = (f32[8,256,256]{2,1,0:T(8,128)}, f32[8,256,256]{2,1,0:T(8,128)}, u32[]{:S(2)}, u32[]{:S(2)}) collective-permute-start(f32[8,256,256]{2,1,0:T(8,128)} %dynamic-slice_bitcast_fusion), channel_id=1, source_target_pairs={{0,32},{32,0},{64,96},{96,64},{128,160},{160,128},{192,224},{224,1... | collective-permute-start | bytes 6291464 | tf_op jit(solution)/shard_map/ppermute | solution.py:44
Sparse Core Ops, SparseCore 0:
  67.8 38.0 reduce-scatter.1

commit v2 on v1

v2 whole, which is shorter than its diff:
```python
import functools

import jax
import jax.numpy as jnp
from jax import lax
from jax.experimental import pallas as pl
from jax.experimental.pallas import tpu as pltpu
from jax.sharding import PartitionSpec as P

ROW_CONTRACT = (((1,), (1,)), ((), ()))
CODE_CONTRACT = (((0,), (0,)), ((), ()))
VMEM = pl.BlockSpec(memory_space=pltpu.VMEM)
SMEM = pl.BlockSpec(memory_space=pltpu.SMEM)
PARAMS = pltpu.CompilerParams(vmem_limit_bytes=40 * 1024 * 1024)


def dot(a, b, contract):
    return lax.dot_general(a, b, contract, preferred_element_type=jnp.float32)


def stats_kernel(tile, lat_ref, up_ref, book_ref, out_ref):
    lat, up = lat_ref[...], up_ref[...]
    tops, totals, weights = [], [], []
    for start in range(0, book_ref.shape[0], tile):
        book = book_ref[start : start + tile, :]
        scores = dot(book, lat, ROW_CONTRACT)
        dprob = dot(book, up, ROW_CONTRACT)
        top = jnp.max(scores, axis=0, keepdims=True)
        expo = jnp.exp(scores - top)
        tops.append(top)
        totals.append(jnp.sum(expo, axis=0, keepdims=True))
        weights.append(jnp.sum(expo * dprob, axis=0, keepdims=True))
    top = functools.reduce(jnp.maximum, tops)
    shares = [jnp.exp(t - top) for t in tops]
    total = sum(s * t for s, t in zip(shares, totals))
    weight = sum(s * w for s, w in zip(shares, weights))
    stats = jnp.concatenate([top, total, weight], axis=0)
    out_ref[...] = jnp.broadcast_to(stats[None], out_ref.shape)


def half_kernel(chunk, where_ref, row_ref, target_ref, lat_ref, up_ref, book_ref, grad_ref, dscore_ref):
    lat, up = lat_ref[...], up_ref[...]
    top, inverse, shift = row_ref[0:1, :], row_ref[1:2, :], row_ref[2:3, :]
    target = target_ref[...]
    codes = lax.broadcasted_iota(jnp.int32, (chunk, lat.shape[0]), 0)
    for pair in range(grad_ref.shape[0] // chunk):
        start = pl.multiple_of((2 * pair + where_ref[0]) * chunk, chunk)
        book = book_ref[pl.ds(start, chunk), :]
        scores = dot(book, lat, ROW_CONTRACT)
        dprob = dot(book, up, ROW_CONTRACT)
        probs = jnp.exp(scores - top) * inverse
        soft = probs * (dprob + shift)
        dscore = jnp.where(codes == target - start, soft - 1.0, soft).astype(jnp.bfloat16)
        here = slice(pair * chunk, (pair + 1) * chunk)
        dscore_ref[here, :] = dscore
        grad_ref[here, :] = dot(dscore, lat, (((1,), (0,)), ((), ()))) + dot(
            probs.astype(jnp.bfloat16), up, (((1,), (0,)), ((), ()))
        )


def latent_kernel(chunk, where_ref, mine_ref, other_ref, book_ref, out_ref):
    total = jnp.zeros((book_ref.shape[1], mine_ref.shape[1]), jnp.float32)
    for pair in range(mine_ref.shape[0] // chunk):
        here = slice(pair * chunk, (pair + 1) * chunk)
        for dscore_ref, side in ((mine_ref, where_ref[0]), (other_ref, 1 - where_ref[0])):
            start = pl.multiple_of((2 * pair + side) * chunk, chunk)
            total += dot(book_ref[pl.ds(start, chunk), :], dscore_ref[here, :], CODE_CONTRACT)
    out_ref[...] = total.T


def shards(latents, upstream, targets, codebook):
    rows, width = latents.shape
    local_codes = codebook.shape[0]
    n_code = lax.axis_size("code")
    n_dp = lax.axis_size("dp")
    chips = n_dp // 2
    chunk = local_codes // n_dp
    core = lax.rem(lax.axis_index("dp"), 2)
    macs = rows * local_codes * width
    f32, bf16 = jnp.float32, jnp.bfloat16

    stats = pl.pallas_call(
        functools.partial(stats_kernel, 512),
        out_shape=jax.ShapeDtypeStruct((n_code, 3, rows), f32),
        in_specs=[VMEM] * 3,
        out_specs=VMEM,
        compiler_params=PARAMS,
        cost_estimate=pl.CostEstimate(
            flops=4 * macs, bytes_accessed=3 << 20, transcendentals=rows * local_codes
        ),
        name="stats",
    )(latents, upstream, codebook)
    every = lax.all_to_all(stats, "code", 0, 0)
    tops = every[:, 0]
    top = jnp.max(tops, axis=0)
    share = jnp.exp(tops - top[None])
    total = jnp.sum(share * every[:, 1], axis=0)
    rowdot = jnp.sum(share * every[:, 2], axis=0) / total
    row = jnp.stack([top, 1.0 / total, 1.0 - rowdot])
    local_target = (targets - lax.axis_index("code") * local_codes)[None]

    half_call = pl.pallas_call(
        functools.partial(half_kernel, chunk),
        out_shape=(
            jax.ShapeDtypeStruct((local_codes // 2, width), f32),
            jax.ShapeDtypeStruct((local_codes // 2, rows), bf16),
        ),
        in_specs=[SMEM] + [VMEM] * 5,
        out_specs=(VMEM, VMEM),
        compiler_params=PARAMS,
        cost_estimate=pl.CostEstimate(
            flops=4 * macs, bytes_accessed=6 << 20, transcendentals=rows * local_codes // 2
        ),
        name="codebook_half",
    )
    away = half_call((1 - core)[None], row, local_target, latents, upstream, codebook)
    got = lax.ppermute(away[0], "dp", [(i, i ^ 1) for i in range(n_dp)])
    mine = half_call(core[None], row, local_target, latents, upstream, codebook)
    groups = [[2 * y + c for y in range(chips)] for c in range(2)]
    codebook_grad = lax.psum_scatter(
        mine[0] + got, "dp", scatter_dimension=0, axis_index_groups=groups, tiled=True
    )
    lat_part = pl.pallas_call(
        functools.partial(latent_kernel, chunk),
        out_shape=jax.ShapeDtypeStruct((rows, width), f32),
        in_specs=[SMEM] + [VMEM] * 3,
        out_specs=VMEM,
        compiler_params=PARAMS,
        cost_estimate=pl.CostEstimate(flops=2 * macs, bytes_accessed=7 << 20, transcendentals=0),
        name="latent_part",
    )(core[None], mine[1], away[1], codebook)
    pieces = lax.all_to_all(lat_part.reshape(n_code, rows // n_code, width), "code", 0, 0)
    piece = jnp.sum(pieces, axis=0)
    latent_grad = lax.all_to_all(
        jnp.broadcast_to(piece[None], (n_code,) + piece.shape), "code", 0, 0
    ).reshape(rows, width)
    return (latent_grad, codebook_grad)


def solution(mesh):
    return jax.shard_map(
        shards,
        mesh=mesh,
        in_specs=(P("dp", None), P("dp", None), P("dp"), P("code", None)),
        out_specs=(P("dp", None), P(("code", "dp"), None)),
        check_vma=False,
    )
```

time: 123 us -> 108 us (0.88)
  the two profiles are of different devices: /device:TPU:56 before, /device:TPU:40 now
where the time goes in v2:
time: 108 us; the launch traced here: 107 us
  blocking collectives  43.8 us (41%)
  starting transfers between devices  15.1 us (14%)
  between operations  14.2 us (13%)
  waiting for transfers between devices  12.6 us (12%)
  Pallas kernels  10.9 us (10%)
  local copies, waits for them, and re-layouts  8.86 us (8%)
  other arithmetic  1.88 us (2%)
    all_to_all x1, blocking collectives, shards(): lax.all_to_all(jnp.broadcast_to(piece[None], (n_code,) + piece.shape), 'c...  22.4 us
    all_to_all x1, blocking collectives, shards(): lax.all_to_all(lat_part.reshape(n_code, rows // n_code, width), 'code', 0...  21.4 us
    all_to_all x1, starting transfers between devices, shards(): every = lax.all_to_all(stats, 'code', 0, 0)  13.2 us
    all_to_all x1, waiting for transfers between devices, shards(): every = lax.all_to_all(stats, 'code', 0, 0)  12.4 us
    unnamed x23, local copies, waits for them, and re-layouts  8.81 us
    pallas_call x1, Pallas kernels, shards(): pl.pallas_call(functools.partial(stats_kernel, 512), out_shape=jax.ShapeD...  4.45 us
    pallas_call x1, Pallas kernels, shards(): half_call((1 - core)[None], row, local_target, latents, upstream, codebook)  2.53 us
    pallas_call x1, Pallas kernels, shards(): mine = half_call(core[None], row, local_target, latents, upstream, codebook)  2.52 us
  transfers between devices with their start and end apart: 3, of which 2 were waited for; matrix products, arithmetic and copies ran while one was open for 0% of the time, Pallas kernels for 4%

profile of v2, /device:TPU:40, one launch (start us, length us, event | category | flops | bytes accessed | tf_op | source)
XLA Modules:
  0.0 107.4 jit_solution(17018821791160900531)
XLA Ops:
  7.2 0.0 copy-start
  7.2 1.6 %copy-done = bf16[4096,256]{1,0:T(8,128)(2,1)S(1)} copy-done((bf16[4096,256]{1,0:T(8,128)(2,1)S(1)}, bf16[4096,256]{1,0:T(8,128)(2,1)}, u32[]{:S(2)}) %copy-start) | copy-done | bytes 2097176
  8.8 0.0 copy-start.6
  8.8 0.9 copy-done.6
  9.7 0.0 copy-start.8
  9.7 0.9 copy-done.8
  10.7 0.0 copy-start.10
  10.7 0.0 copy-start.1
  10.7 0.0 copy-start.7
  10.7 0.0 copy-start.9
  10.7 4.5 %stats.1 = f32[32,3,512]{2,1,0:T(4,128)} custom-call(bf16[512,256]{1,0:T(8,128)(2,1)S(1)} %copy-done.6, bf16[512,256]{1,0:T(8,128)(2,1)S(1)} %copy-done.8, bf16[4096,256]{1,0:T(8,128)(2,1)S(1)} %copy-done), custom_call_target="tpu_custom_call" | custom-call | flops 2147483648 | bytes 3145728 | tf_op jit(solution)/shard_map/stats/pallas_call | solution.py:82
  15.1 13.2 %all-to-all-start = ((f32[32,3,512]{2,1,0:T(4,128)}), f32[32,3,512]{2,1,0:T(4,128)S(1)}, u32[]{:S(2)}, u32[]{:S(2)}) async-start(f32[32,3,512]{2,1,0:T(4,128)} %stats.1), calls=%async_computation | async-start | bytes 524288 | tf_op jit(solution)/shard_map/all_to_all | solution.py:93
  28.3 0.0 reduce-scatter.2.cloned.1.call-start
  28.4 0.0 copy-done.10
  28.4 12.4 %all-to-all-done = f32[32,3,512]{2,1,0:T(4,128)S(1)} async-done(((f32[32,3,512]{2,1,0:T(4,128)}), f32[32,3,512]{2,1,0:T(4,128)S(1)}, u32[]{:S(2)}, u32[]{:S(2)}) %all-to-all-start) | async-done | bytes 196640 | tf_op jit(solution)/shard_map/all_to_all | solution.py:93
  40.8 0.2 fusion.5
  41.0 0.0 copy-done.1
  41.0 0.0 copy-done.7
  41.0 0.0 copy-done.9
  41.0 2.5 %codebook_half.3 = (f32[2048,256]{1,0:T(8,128)S(1)}, bf16[2048,512]{1,0:T(8,128)(2,1)S(1)}) custom-call(s32[1]{0:T(128)} %bitcast.7.where_ref, f32[3,512]{1,0:T(4,128)S(1)} %pad_maximum_fusion.row_ref, s32[1,512]{1,0:T(1,128)S(1)} %bitcast.29, bf16[512,256]{1,0:T(8,128)(2,1)S(1)} %copy-done.7, bf16[512,256]{1,0:T(8,128)(2,1)S(1)} %copy-done.9, ...), custom_call_target="tpu_custom_call" | custom-call | flops 2147483648 | bytes 6291456 | tf_op jit(solution)/shard_map/codebook_half/pallas_call | solution.py:116
  43.6 0.0 copy-start.2
  43.6 1.9 %collective-permute-start = (f32[2048,256]{1,0:T(8,128)S(1)}, f32[2048,256]{1,0:T(8,128)S(1)}, u32[]{:S(2)}, u32[]{:S(2)}) collective-permute-start(f32[2048,256]{1,0:T(8,128)S(1)} %get-tuple-element.9), channel_id=1, source_target_pairs={{0,32},{32,0},{64,96},{96,64},{128,160},{160,128},{192,224},{224,1... | collective-permute-start | bytes 6291464 | tf_op jit(solution)/shard_map/ppermute | solution.py:117
  45.5 2.5 %codebook_half.2 = (f32[2048,256]{1,0:T(8,128)S(1)}, bf16[2048,512]{1,0:T(8,128)(2,1)S(1)}) custom-call(s32[1]{0:T(128)} %bitcast.where_ref, f32[3,512]{1,0:T(4,128)S(1)} %pad_maximum_fusion.row_ref, s32[1,512]{1,0:T(1,128)S(1)} %bitcast.30, bf16[512,256]{1,0:T(8,128)(2,1)S(1)} %copy-done.7, bf16[512,256]{1,0:T(8,128)(2,1)S(1)} %copy-done.9, ...), custom_call_target="tpu_custom_call" | custom-call | flops 2147483648 | bytes 6291456 | tf_op jit(solution)/shard_map/codebook_half/pallas_call | solution.py:118
  48.0 0.0 copy-done.2
  48.1 0.0 copy-start.4
  48.1 1.3 %copy-done.4 = bf16[2048,512]{1,0:T(8,128)(2,1)} copy-done((bf16[2048,512]{1,0:T(8,128)(2,1)}, bf16[2048,512]{1,0:T(8,128)(2,1)S(1)}, u32[]{:S(2)}) %copy-start.4) | copy-done | bytes 2097176
  49.4 0.2 collective-permute-done
  49.6 1.6 %add.5 = f32[2048,256]{1,0:T(8,128)} add(f32[2048,256]{1,0:T(8,128)S(1)} %get-tuple-element.8, f32[2048,256]{1,0:T(8,128)S(1)} %collective-permute-done) | non-fusion elementwise | flops 524288 | bytes 6291456 | tf_op jit(solution)/shard_map/add | solution.py:121
  51.2 0.0 reduce-scatter.2.cloned.1.call-update
  51.3 0.0 copy-start.3
  51.3 1.6 %copy-done.3 = bf16[2048,512]{1,0:T(8,128)(2,1)S(1)} copy-done((bf16[2048,512]{1,0:T(8,128)(2,1)S(1)}, bf16[2048,512]{1,0:T(8,128)(2,1)}, u32[]{:S(2)}) %copy-start.3) | copy-done | bytes 2097176
  52.9 0.0 copy-start.5
  52.9 1.6 %copy-done.5 = bf16[2048,512]{1,0:T(8,128)(2,1)S(1)} copy-done((bf16[2048,512]{1,0:T(8,128)(2,1)S(1)}, bf16[2048,512]{1,0:T(8,128)(2,1)}, u32[]{:S(2)}) %copy-start.5) | copy-done | bytes 2097176
  54.5 1.4 %latent_part.1 = f32[512,256]{1,0:T(8,128)S(1)} custom-call(s32[1]{0:T(128)} %bitcast.where_ref, bf16[2048,512]{1,0:T(8,128)(2,1)S(1)} %copy-done.5, bf16[2048,512]{1,0:T(8,128)(2,1)S(1)} %copy-done.3, bf16[4096,256]{1,0:T(8,128)(2,1)S(1)} %copy-done.1), custom_call_target="tpu_custom_call" | custom-call | flops 1073741824 | bytes 7340032 | tf_op jit(solution)/shard_map/latent_part/pallas_call | solution.py:123
  55.9 21.4 %all_to_all.15 = f32[32,16,256]{2,1,0:T(8,128)S(1)} all-to-all(f32[32,16,256]{2,1,0:T(8,128)S(1)} %bitcast.28), channel_id=1, replica_groups=mesh['dp'=16,'code'=32] {'code'}, dimensions={0} | all-to-all | bytes 1048576 | tf_op jit(solution)/shard_map/all_to_all | solution.py:132
  77.3 0.1 broadcast_in_dim.20
  77.3 22.4 %all_to_all.16 = f32[32,16,256]{2,1,0:T(8,128)S(1)} all-to-all(f32[32,16,256]{2,1,0:T(8,128)S(1)} %broadcast_in_dim.20), channel_id=1, replica_groups=mesh['dp'=16,'code'=32] {'code'}, dimensions={0} | all-to-all | bytes 1048576 | tf_op jit(solution)/shard_map/all_to_all | solution.py:134
  99.8 0.0 reduce-scatter.2.cloned.1.call-done
  99.8 0.8 copy.28
  (5 shorter events, 0.1 us)
Async XLA Ops:
  7.2 1.6 %copy-start = (bf16[4096,256]{1,0:T(8,128)(2,1)S(1)}, bf16[4096,256]{1,0:T(8,128)(2,1)}, u32[]{:S(2)}) copy-start(bf16[4096,256]{1,0:T(8,128)(2,1)} %book_ref.7) | copy-start | bytes 6291460
  8.8 0.9 copy-start.6
  9.7 0.9 copy-start.8
  10.7 17.7 %copy-start.10 = (s32[512]{0:T(512)S(1)}, s32[512]{0:T(512)}, u32[]{:S(2)}) copy-start(s32[512]{0:T(512)} %param.6) | copy-start | bytes 6148
  10.7 30.4 %copy-start.1 = (bf16[4096,256]{1,0:T(8,128)(2,1)S(1)}, bf16[4096,256]{1,0:T(8,128)(2,1)}, u32[]{:S(2)}) copy-start(bf16[4096,256]{1,0:T(8,128)(2,1)} %book_ref.7) | copy-start | bytes 6291460
  10.7 30.4 %copy-start.7 = (bf16[512,256]{1,0:T(8,128)(2,1)S(1)}, bf16[512,256]{1,0:T(8,128)(2,1)}, u32[]{:S(2)}) copy-start(bf16[512,256]{1,0:T(8,128)(2,1)} %lat_ref.5) | copy-start | bytes 786436
  10.7 30.4 %copy-start.9 = (bf16[512,256]{1,0:T(8,128)(2,1)S(1)}, bf16[512,256]{1,0:T(8,128)(2,1)}, u32[]{:S(2)}) copy-start(bf16[512,256]{1,0:T(8,128)(2,1)} %up_ref.5) | copy-start | bytes 786436
  15.1 25.6 %all-to-all-start = ((f32[32,3,512]{2,1,0:T(4,128)}), f32[32,3,512]{2,1,0:T(4,128)S(1)}, u32[]{:S(2)}, u32[]{:S(2)}) async-start(f32[32,3,512]{2,1,0:T(4,128)} %stats.1), calls=%async_computation | async-start | bytes 524288 | tf_op jit(solution)/shard_map/all_to_all | solution.py:93
  28.3 71.4 %reduce-scatter.2.cloned.1.call-start = ((), (), s32[]{:S(2)}) async-start(), calls=%async_computation.4 | async-start | bytes 2359296 | tf_op jit(solution)/shard_map/reduce_scatter | solution.py:120
  43.6 4.5 %copy-start.2 = (bf16[2048,512]{1,0:T(8,128)(2,1)}, bf16[2048,512]{1,0:T(8,128)(2,1)S(1)}, u32[]{:S(2)}) copy-start(bf16[2048,512]{1,0:T(8,128)(2,1)S(1)} %get-tuple-element.7.other_ref) | copy-start | bytes 6291460
  43.6 6.1 %collective-permute-start = (f32[2048,256]{1,0:T(8,128)S(1)}, f32[2048,256]{1,0:T(8,128)S(1)}, u32[]{:S(2)}, u32[]{:S(2)}) collective-permute-start(f32[2048,256]{1,0:T(8,128)S(1)} %get-tuple-element.9), channel_id=1, source_target_pairs={{0,32},{32,0},{64,96},{96,64},{128,160},{160,128},{192,224},{224,1... | collective-permute-start | bytes 6291464 | tf_op jit(solution)/shard_map/ppermute | solution.py:117
  48.1 1.3 %copy-start.4 = (bf16[2048,512]{1,0:T(8,128)(2,1)}, bf16[2048,512]{1,0:T(8,128)(2,1)S(1)}, u32[]{:S(2)}) copy-start(bf16[2048,512]{1,0:T(8,128)(2,1)S(1)} %get-tuple-element.6.mine_ref) | copy-start | bytes 6291460
  51.3 1.6 %copy-start.3 = (bf16[2048,512]{1,0:T(8,128)(2,1)S(1)}, bf16[2048,512]{1,0:T(8,128)(2,1)}, u32[]{:S(2)}) copy-start(bf16[2048,512]{1,0:T(8,128)(2,1)} %copy-done.2) | copy-start | bytes 6291460
  52.9 1.6 %copy-start.5 = (bf16[2048,512]{1,0:T(8,128)(2,1)S(1)}, bf16[2048,512]{1,0:T(8,128)(2,1)}, u32[]{:S(2)}) copy-start(bf16[2048,512]{1,0:T(8,128)(2,1)} %copy-done.4) | copy-start | bytes 6291460
Sparse Core Ops, SparseCore 0:
  51.4 38.7 reduce-scatter.1

commit v3 on v2

--- a/solution.py
+++ b/solution.py
@@ -9,22 +9,37 @@
 
 ROW_CONTRACT = (((1,), (1,)), ((), ()))
 CODE_CONTRACT = (((0,), (0,)), ((), ()))
+PLAIN = (((1,), (0,)), ((), ()))
 VMEM = pl.BlockSpec(memory_space=pltpu.VMEM)
 SMEM = pl.BlockSpec(memory_space=pltpu.SMEM)
-PARAMS = pltpu.CompilerParams(vmem_limit_bytes=40 * 1024 * 1024)
+HBM = pl.BlockSpec(memory_space=pltpu.HBM)
+PARAMS = pltpu.CompilerParams(vmem_limit_bytes=24 * 1024 * 1024)
 
 
 def dot(a, b, contract):
     return lax.dot_general(a, b, contract, preferred_element_type=jnp.float32)
 
 
-def stats_kernel(tile, lat_ref, up_ref, book_ref, out_ref):
-    lat, up = lat_ref[...], up_ref[...]
+def stats_kernel(tile, lat_hbm, up_hbm, book_hbm, out_ref, lat_ref, up_ref, book_ref, sems):
+    starts = range(0, book_hbm.shape[0], tile)
+    loads = [pltpu.make_async_copy(lat_hbm, lat_ref, sems.at[0])]
+    for n, start in enumerate(starts):
+        part = pl.ds(start, tile)
+        loads.append(pltpu.make_async_copy(book_hbm.at[part], book_ref.at[part], sems.at[n + 1]))
+    loads.insert(2, pltpu.make_async_copy(up_hbm, up_ref, sems.at[len(loads)]))
+    for load in loads:
+        load.start()
+    loads[0].wait()
     tops, totals, weights = [], [], []
-    for start in range(0, book_ref.shape[0], tile):
+    for n, start in enumerate(starts):
+        if n == 0:
+            loads[1].wait()
+            loads[2].wait()
+        else:
+            loads[n + 2].wait()
         book = book_ref[start : start + tile, :]
-        scores = dot(book, lat, ROW_CONTRACT)
-        dprob = dot(book, up, ROW_CONTRACT)
+        scores = dot(book, lat_ref[...], ROW_CONTRACT)
+        dprob = dot(book, up_ref[...], ROW_CONTRACT)
         top = jnp.max(scores, axis=0, keepdims=True)
         expo = jnp.exp(scores - top)
         tops.append(top)
@@ -38,32 +53,41 @@
     out_ref[...] = jnp.broadcast_to(stats[None], out_ref.shape)
 
 
+def chunk_ids(chips, y, core):
+    step = 1 - 2 * core
+    ids = []
+    for far in range(1, chips // 2):
+        chip = lax.rem(y + far * step + chips, chips)
+        ids += [2 * chip + core, 2 * chip + 1 - core]
+    return ids + [2 * lax.rem(y + chips // 2, chips) + core, 2 * y + core]
+
+
 def half_kernel(chunk, where_ref, row_ref, target_ref, lat_ref, up_ref, book_ref, grad_ref, dscore_ref):
     lat, up = lat_ref[...], up_ref[...]
     top, inverse, shift = row_ref[0:1, :], row_ref[1:2, :], row_ref[2:3, :]
     target = target_ref[...]
     codes = lax.broadcasted_iota(jnp.int32, (chunk, lat.shape[0]), 0)
-    for pair in range(grad_ref.shape[0] // chunk):
-        start = pl.multiple_of((2 * pair + where_ref[0]) * chunk, chunk)
+    ids = chunk_ids(book_ref.shape[0] // chunk // 2, where_ref[0], where_ref[1])
+    for n, which in enumerate(ids):
+        start = pl.multiple_of(which * chunk, chunk)
         book = book_ref[pl.ds(start, chunk), :]
         scores = dot(book, lat, ROW_CONTRACT)
         dprob = dot(book, up, ROW_CONTRACT)
         probs = jnp.exp(scores - top) * inverse
         soft = probs * (dprob + shift)
         dscore = jnp.where(codes == target - start, soft - 1.0, soft).astype(jnp.bfloat16)
-        here = slice(pair * chunk, (pair + 1) * chunk)
+        here = slice(n * chunk, (n + 1) * chunk)
         dscore_ref[here, :] = dscore
-        grad_ref[here, :] = dot(dscore, lat, (((1,), (0,)), ((), ()))) + dot(
-            probs.astype(jnp.bfloat16), up, (((1,), (0,)), ((), ()))
-        )
+        grad_ref[here, :] = dot(dscore, lat, PLAIN) + dot(probs.astype(jnp.bfloat16), up, PLAIN)
 
 
 def latent_kernel(chunk, where_ref, mine_ref, other_ref, book_ref, out_ref):
     total = jnp.zeros((book_ref.shape[1], mine_ref.shape[1]), jnp.float32)
-    for pair in range(mine_ref.shape[0] // chunk):
-        here = slice(pair * chunk, (pair + 1) * chunk)
-        for dscore_ref, side in ((mine_ref, where_ref[0]), (other_ref, 1 - where_ref[0])):
-            start = pl.multiple_of((2 * pair + side) * chunk, chunk)
+    chips = book_ref.shape[0] // chunk // 2
+    for dscore_ref, core in ((mine_ref, where_ref[1]), (other_ref, 1 - where_ref[1])):
+        for n, which in enumerate(chunk_ids(chips, where_ref[0], core)):
+            start = pl.multiple_of(which * chunk, chunk)
+            here = slice(n * chunk, (n + 1) * chunk)
             total += dot(book_ref[pl.ds(start, chunk), :], dscore_ref[here, :], CODE_CONTRACT)
     out_ref[...] = total.T
 
@@ -75,16 +99,24 @@
     n_dp = lax.axis_size("dp")
     chips = n_dp // 2
     chunk = local_codes // n_dp
-    core = lax.rem(lax.axis_index("dp"), 2)
+    here = lax.axis_index("dp")
+    y, core = here // 2, lax.rem(here, 2)
     macs = rows * local_codes * width
     f32, bf16 = jnp.float32, jnp.bfloat16
 
+    tile = 512
     stats = pl.pallas_call(
-        functools.partial(stats_kernel, 512),
+        functools.partial(stats_kernel, tile),
         out_shape=jax.ShapeDtypeStruct((n_code, 3, rows), f32),
-        in_specs=[VMEM] * 3,
+        in_specs=[HBM] * 3,
         out_specs=VMEM,
-        compiler_params=PARAMS,
+        scratch_shapes=[
+            pltpu.VMEM((rows, width), bf16),
+            pltpu.VMEM((rows, width), bf16),
+            pltpu.VMEM((local_codes, width), bf16),
+            pltpu.SemaphoreType.DMA((local_codes // tile + 2,)),
+        ],
+        compiler_params=pltpu.CompilerParams(vmem_limit_bytes=60 * 1024 * 1024),
         cost_estimate=pl.CostEstimate(
             flops=4 * macs, bytes_accessed=3 << 20, transcendentals=rows * local_codes
         ),
@@ -113,13 +145,9 @@
         ),
         name="codebook_half",
     )
-    away = half_call((1 - core)[None], row, local_target, latents, upstream, codebook)
+    away = half_call(jnp.stack([y, 1 - core]), row, local_target, latents, upstream, codebook)
     got = lax.ppermute(away[0], "dp", [(i, i ^ 1) for i in range(n_dp)])
-    mine = half_call(core[None], row, local_target, latents, upstream, codebook)
-    groups = [[2 * y + c for y in range(chips)] for c in range(2)]
-    codebook_grad = lax.psum_scatter(
-        mine[0] + got, "dp", scatter_dimension=0, axis_index_groups=groups, tiled=True
-    )
+    mine = half_call(jnp.stack([y, core]), row, local_target, latents, upstream, codebook)
     lat_part = pl.pallas_call(
         functools.partial(latent_kernel, chunk),
         out_shape=jax.ShapeDtypeStruct((rows, width), f32),
@@ -128,12 +156,45 @@
         compiler_params=PARAMS,
         cost_estimate=pl.CostEstimate(flops=2 * macs, bytes_accessed=7 << 20, transcendentals=0),
         name="latent_part",
-    )(core[None], mine[1], away[1], codebook)
+    )(jnp.stack([y, core]), mine[1], away[1], codebook)
+    half, lat_part = lax.optimization_barrier((mine[0], lat_part))
+
+    def along(far):
+        return [
+            (i, (i // 2 + far * (1 - 2 * (i % 2))) % chips * 2 + i % 2) for i in range(n_dp)
+        ]
+
+    near, middle, far, across, own = [
+        half[at : at + size] + got[at : at + size]
+        for at, size in (
+            (0, 2 * chunk),
+            (2 * chunk, 2 * chunk),
+            (4 * chunk, 2 * chunk),
+            (6 * chunk, chunk),
+            (7 * chunk, chunk),
+        )
+    ]
+    near, middle, far, across, own, lat_part = lax.optimization_barrier(
+        (near, middle, far, across, own, lat_part)
+    )
+    far_came = lax.ppermute(far, "dp", along(1))
+    across_came = lax.ppermute(across, "dp", along(2))
+    near_came = lax.ppermute(near, "dp", along(1))
+    merged = jnp.concatenate(
+        [middle[:chunk] + far_came[:chunk] + across_came, middle[chunk:] + far_came[chunk:]]
+    )
+    merged_came = lax.ppermute(merged, "dp", along(2))
+
     pieces = lax.all_to_all(lat_part.reshape(n_code, rows // n_code, width), "code", 0, 0)
     piece = jnp.sum(pieces, axis=0)
     latent_grad = lax.all_to_all(
         jnp.broadcast_to(piece[None], (n_code,) + piece.shape), "code", 0, 0
     ).reshape(rows, width)
+
+    last = lax.ppermute(
+        near_came[chunk:] + merged_came[chunk:], "dp", [(i, i ^ 1) for i in range(n_dp)]
+    )
+    codebook_grad = near_came[:chunk] + merged_came[:chunk] + own + last
     return (latent_grad, codebook_grad)
 
 

time: 108 us -> 99.3 us (0.919)
  the two profiles are of different devices: /device:TPU:40 before, /device:TPU:72 now
where the time goes in v3:
time: 99.3 us; the launch traced here: 98.7 us
  starting transfers between devices  46.1 us (46%)
  waiting for transfers between devices  32.4 us (33%)
  Pallas kernels  15.4 us (16%)
  other arithmetic  2.25 us (2%)
  local copies, waits for them, and re-layouts  1.66 us (2%)
    all_to_all x1, starting transfers between devices, shards(): every = lax.all_to_all(stats, 'code', 0, 0)  12.6 us
    all_to_all x1, waiting for transfers between devices, shards(): every = lax.all_to_all(stats, 'code', 0, 0)  12.2 us
    all_to_all x1, starting transfers between devices, shards(): lax.all_to_all(jnp.broadcast_to(piece[None], (n_code,) + piece.shape), 'c...  9.78 us
    all_to_all x1, waiting for transfers between devices, shards(): lax.all_to_all(jnp.broadcast_to(piece[None], (n_code,) + piece.shape), 'c...  9.39 us
    pallas_call x1, Pallas kernels, shards(): pl.pallas_call(functools.partial(stats_kernel, tile), out_shape=jax.Shape...  6.59 us
    ppermute x1, starting transfers between devices, shards(): across_came = lax.ppermute(across, 'dp', along(2))  5.71 us
    ppermute x1, waiting for transfers between devices, shards(): across_came = lax.ppermute(across, 'dp', along(2))  5 us
    all_to_all x1, starting transfers between devices, shards(): lax.all_to_all(lat_part.reshape(n_code, rows // n_code, width), 'code', 0...  4.58 us
  transfers between devices with their start and end apart: 9, of which 5 were waited for; matrix products, arithmetic and copies ran while one was open for 2% of the time, Pallas kernels for 6%

profile of v3, /device:TPU:72, one launch (start us, length us, event | category | flops | bytes accessed | tf_op | source)
XLA Modules:
  0.0 98.7 jit_solution(1449293182487439702)
XLA Ops:
  0.6 0.0 copy-start.1
  0.6 0.0 copy-start.2
  0.7 0.0 copy-start
  0.7 0.0 copy-start.3
  0.7 6.6 %stats.1 = f32[32,3,512]{2,1,0:T(4,128)} custom-call(bf16[512,256]{1,0:T(8,128)(2,1)} %lat_ref.3, bf16[512,256]{1,0:T(8,128)(2,1)} %up_ref.3, bf16[4096,256]{1,0:T(8,128)(2,1)} %book_ref.5), custom_call_target="tpu_custom_call" | custom-call | flops 2147483648 | bytes 3145728 | tf_op jit(solution)/shard_map/stats/pallas_call | solution.py:108
  7.3 12.6 %all-to-all-start = ((f32[32,3,512]{2,1,0:T(4,128)}), f32[32,3,512]{2,1,0:T(4,128)S(1)}, u32[]{:S(2)}, u32[]{:S(2)}) async-start(f32[32,3,512]{2,1,0:T(4,128)} %stats.1), calls=%async_computation | async-start | bytes 524288 | tf_op jit(solution)/shard_map/all_to_all | solution.py:125
  19.9 0.1 pad_add_fusion
  20.0 0.0 copy-done.3
  20.0 12.2 %all-to-all-done = f32[32,3,512]{2,1,0:T(4,128)S(1)} async-done(((f32[32,3,512]{2,1,0:T(4,128)}), f32[32,3,512]{2,1,0:T(4,128)S(1)}, u32[]{:S(2)}, u32[]{:S(2)}) %all-to-all-start) | async-done | bytes 196640 | tf_op jit(solution)/shard_map/all_to_all | solution.py:125
  32.2 0.2 fusion.8
  32.4 0.0 copy-done.1
  32.4 0.0 copy-done.2
  32.4 0.0 copy-done
  32.4 3.0 %codebook_half.3 = (f32[2048,256]{1,0:T(8,128)S(1)}, bf16[2048,512]{1,0:T(8,128)(2,1)S(1)}) custom-call(s32[2]{0:T(128)S(1)} %get-tuple-element.42.where_ref, f32[3,512]{1,0:T(4,128)S(1)} %pad_maximum_fusion.1.row_ref, s32[1,512]{1,0:T(1,128)S(1)} %bitcast.29, bf16[512,256]{1,0:T(8,128)(2,1)S(1)} %copy-done.1, bf16[512,256]{1,0:T(8,128)(2,1)S(1)} %copy-done.2, ...), custom_call_target="tpu_custom_call" | custom-call | flops 2147483648 | bytes 6291456 | tf_op jit(solution)/shard_map/codebook_half/pallas_call | solution.py:148
  35.5 1.9 %collective-permute-start = (f32[2048,256]{1,0:T(8,128)S(1)}, f32[2048,256]{1,0:T(8,128)S(1)}, u32[]{:S(2)}, u32[]{:S(2)}) collective-permute-start(f32[2048,256]{1,0:T(8,128)S(1)} %get-tuple-element.18), channel_id=1, source_target_pairs={{0,32},{32,0},{64,96},{96,64},{128,160},{160,128},{192,224},{224,1... | collective-permute-start | bytes 6291464 | tf_op jit(solution)/shard_map/ppermute | solution.py:149
  37.4 3.0 %codebook_half.2 = (f32[2048,256]{1,0:T(8,128)S(1)}, bf16[2048,512]{1,0:T(8,128)(2,1)S(1)}) custom-call(s32[2]{0:T(128)S(1)} %get-tuple-element.41.where_ref, f32[3,512]{1,0:T(4,128)S(1)} %pad_maximum_fusion.1.row_ref, s32[1,512]{1,0:T(1,128)S(1)} %bitcast.30, bf16[512,256]{1,0:T(8,128)(2,1)S(1)} %copy-done.1, bf16[512,256]{1,0:T(8,128)(2,1)S(1)} %copy-done.2, ...), custom_call_target="tpu_custom_call" | custom-call | flops 2147483648 | bytes 6291456 | tf_op jit(solution)/shard_map/codebook_half/pallas_call | solution.py:150
  40.4 2.7 %latent_part.1 = f32[512,256]{1,0:T(8,128)} custom-call(s32[2]{0:T(128)S(1)} %get-tuple-element.41.where_ref, bf16[2048,512]{1,0:T(8,128)(2,1)S(1)} %get-tuple-element.15.mine_ref, bf16[2048,512]{1,0:T(8,128)(2,1)S(1)} %get-tuple-element.16.other_ref, bf16[4096,256]{1,0:T(8,128)(2,1)S(1)} %copy-done), custom_call_target="tpu_custom_call" | custom-call | flops 1073741824 | bytes 7340032 | tf_op jit(solution)/shard_map/latent_part/pallas_call | solution.py:151
  43.2 0.0 collective-permute-done
  43.2 0.2 slice_add_fusion
  43.4 0.8 slice_add_fusion.7
  44.2 3.5 %collective-permute-start.2 = (f32[512,256]{1,0:T(8,128)S(1)}, f32[512,256]{1,0:T(8,128)S(1)}, u32[]{:S(2)}, u32[]{:S(2)}) collective-permute-start(f32[512,256]{1,0:T(8,128)S(1)} %get-tuple-element.23), channel_id=1, source_target_pairs={{0,64},{32,480},{64,128},{96,32},{128,192},{160,96},{192,256},{224... | collective-permute-start | bytes 1572872 | tf_op jit(solution)/shard_map/ppermute | solution.py:180
  47.7 4.6 %all-to-all-start.1 = ((f32[32,16,256]{2,1,0:T(8,128)}), f32[32,16,256]{2,1,0:T(8,128)S(1)}, u32[]{:S(2)}, u32[]{:S(2)}) async-start(f32[32,16,256]{2,1,0:T(8,128)} %bitcast.9), calls=%async_computation.1 | async-start | bytes 1048576 | tf_op jit(solution)/shard_map/all_to_all | solution.py:188
  52.2 5.7 %collective-permute-start.3 = (f32[256,256]{1,0:T(8,128)}, f32[256,256]{1,0:T(8,128)S(1)}, u32[]{:S(2)}, u32[]{:S(2)}) collective-permute-start(f32[256,256]{1,0:T(8,128)} %get-tuple-element.24), channel_id=1, source_target_pairs={{0,128},{32,416},{64,192},{96,480},{128,256},{160,32},{192,320},{2... | collective-permute-start | bytes 786440 | tf_op jit(solution)/shard_map/ppermute | solution.py:181
  58.0 2.6 %collective-permute-start.1 = (f32[512,256]{1,0:T(8,128)S(1)}, f32[512,256]{1,0:T(8,128)S(1)}, u32[]{:S(2)}, u32[]{:S(2)}) collective-permute-start(f32[512,256]{1,0:T(8,128)S(1)} %get-tuple-element.21), channel_id=1, source_target_pairs={{0,64},{32,480},{64,128},{96,32},{128,192},{160,96},{192,256},{224... | collective-permute-start | bytes 1572872 | tf_op jit(solution)/shard_map/ppermute | solution.py:182
  60.5 5.0 %collective-permute-done.3 = f32[256,256]{1,0:T(8,128)S(1)} collective-permute-done((f32[256,256]{1,0:T(8,128)}, f32[256,256]{1,0:T(8,128)S(1)}, u32[]{:S(2)}, u32[]{:S(2)}) %collective-permute-start.3) | collective-permute-done | bytes 262176 | tf_op jit(solution)/shard_map/ppermute | solution.py:181
  65.6 0.0 collective-permute-done.2
  65.6 0.1 fusion.2
  65.7 3.5 %collective-permute-start.4 = (f32[512,256]{1,0:T(8,128)S(1)}, f32[512,256]{1,0:T(8,128)S(1)}, u32[]{:S(2)}, u32[]{:S(2)}) collective-permute-start(f32[512,256]{1,0:T(8,128)S(1)} %pad_maximum_fusion), channel_id=1, source_target_pairs={{0,128},{32,416},{64,192},{96,480},{128,256},{160,32},{192,320},{2... | collective-permute-start | bytes 1572872 | tf_op jit(solution)/shard_map/ppermute | solution.py:186
  69.2 0.0 all-to-all-done.1
  69.3 0.9 broadcast_in_dim.5
  70.1 9.8 %all-to-all-start.2 = ((f32[32,16,256]{2,1,0:T(8,128)}), f32[32,16,256]{2,1,0:T(8,128)S(1)}, u32[]{:S(2)}, u32[]{:S(2)}) async-start(f32[32,16,256]{2,1,0:T(8,128)} %broadcast_in_dim.5), calls=%async_computation.2 | async-start | bytes 1048576 | tf_op jit(solution)/shard_map/all_to_all | solution.py:190
  79.9 0.0 collective-permute-done.1
  79.9 4.3 %collective-permute-done.4 = f32[512,256]{1,0:T(8,128)S(1)} collective-permute-done((f32[512,256]{1,0:T(8,128)S(1)}, f32[512,256]{1,0:T(8,128)S(1)}, u32[]{:S(2)}, u32[]{:S(2)}) %collective-permute-start.4) | collective-permute-done | bytes 524320 | tf_op jit(solution)/shard_map/ppermute | solution.py:186
  84.3 1.9 %collective-permute-start.5 = (f32[256,256]{1,0:T(8,128)S(1)}, f32[256,256]{1,0:T(8,128)S(1)}, u32[]{:S(2)}, u32[]{:S(2)}) collective-permute-start(f32[256,256]{1,0:T(8,128)S(1)} %slice_add_fusion.3), channel_id=1, source_target_pairs={{0,32},{32,0},{64,96},{96,64},{128,160},{160,128},{192,224},{224,1... | collective-permute-start | bytes 786440 | tf_op jit(solution)/shard_map/ppermute | solution.py:194
  86.2 1.5 %collective-permute-done.5 = f32[256,256]{1,0:T(8,128)S(1)} collective-permute-done((f32[256,256]{1,0:T(8,128)S(1)}, f32[256,256]{1,0:T(8,128)S(1)}, u32[]{:S(2)}, u32[]{:S(2)}) %collective-permute-start.5) | collective-permute-done | bytes 262176 | tf_op jit(solution)/shard_map/ppermute | solution.py:194
  87.7 0.8 fusion.1
  88.5 9.4 %all-to-all-done.2 = f32[32,16,256]{2,1,0:T(8,128)S(1)} async-done(((f32[32,16,256]{2,1,0:T(8,128)}), f32[32,16,256]{2,1,0:T(8,128)S(1)}, u32[]{:S(2)}, u32[]{:S(2)}) %all-to-all-start.2) | async-done | bytes 524320 | tf_op jit(solution)/shard_map/all_to_all | solution.py:190
  97.9 0.8 copy.28
  (7 shorter events, 0.2 us)
Async XLA Ops:
  0.6 31.8 %copy-start.1 = (bf16[512,256]{1,0:T(8,128)(2,1)S(1)}, bf16[512,256]{1,0:T(8,128)(2,1)}, u32[]{:S(2)}) copy-start(bf16[512,256]{1,0:T(8,128)(2,1)} %lat_ref.3) | copy-start | bytes 786436
  0.6 31.8 %copy-start.2 = (bf16[512,256]{1,0:T(8,128)(2,1)S(1)}, bf16[512,256]{1,0:T(8,128)(2,1)}, u32[]{:S(2)}) copy-start(bf16[512,256]{1,0:T(8,128)(2,1)} %up_ref.3) | copy-start | bytes 786436
  0.7 31.8 %copy-start = (bf16[4096,256]{1,0:T(8,128)(2,1)S(1)}, bf16[4096,256]{1,0:T(8,128)(2,1)}, u32[]{:S(2)}) copy-start(bf16[4096,256]{1,0:T(8,128)(2,1)} %book_ref.5) | copy-start | bytes 6291460
  0.7 19.3 %copy-start.3 = (s32[512]{0:T(512)S(1)}, s32[512]{0:T(512)}, u32[]{:S(2)}) copy-start(s32[512]{0:T(512)} %param.6) | copy-start | bytes 6148
  7.3 24.9 %all-to-all-start = ((f32[32,3,512]{2,1,0:T(4,128)}), f32[32,3,512]{2,1,0:T(4,128)S(1)}, u32[]{:S(2)}, u32[]{:S(2)}) async-start(f32[32,3,512]{2,1,0:T(4,128)} %stats.1), calls=%async_computation | async-start | bytes 524288 | tf_op jit(solution)/shard_map/all_to_all | solution.py:125
  35.5 7.7 %collective-permute-start = (f32[2048,256]{1,0:T(8,128)S(1)}, f32[2048,256]{1,0:T(8,128)S(1)}, u32[]{:S(2)}, u32[]{:S(2)}) collective-permute-start(f32[2048,256]{1,0:T(8,128)S(1)} %get-tuple-element.18), channel_id=1, source_target_pairs={{0,32},{32,0},{64,96},{96,64},{128,160},{160,128},{192,224},{224,1... | collective-permute-start | bytes 6291464 | tf_op jit(solution)/shard_map/ppermute | solution.py:149
  44.2 21.4 %collective-permute-start.2 = (f32[512,256]{1,0:T(8,128)S(1)}, f32[512,256]{1,0:T(8,128)S(1)}, u32[]{:S(2)}, u32[]{:S(2)}) collective-permute-start(f32[512,256]{1,0:T(8,128)S(1)} %get-tuple-element.23), channel_id=1, source_target_pairs={{0,64},{32,480},{64,128},{96,32},{128,192},{160,96},{192,256},{224... | collective-permute-start | bytes 1572872 | tf_op jit(solution)/shard_map/ppermute | solution.py:180
  47.7 21.6 %all-to-all-start.1 = ((f32[32,16,256]{2,1,0:T(8,128)}), f32[32,16,256]{2,1,0:T(8,128)S(1)}, u32[]{:S(2)}, u32[]{:S(2)}) async-start(f32[32,16,256]{2,1,0:T(8,128)} %bitcast.9), calls=%async_computation.1 | async-start | bytes 1048576 | tf_op jit(solution)/shard_map/all_to_all | solution.py:188
  52.2 13.3 %collective-permute-start.3 = (f32[256,256]{1,0:T(8,128)}, f32[256,256]{1,0:T(8,128)S(1)}, u32[]{:S(2)}, u32[]{:S(2)}) collective-permute-start(f32[256,256]{1,0:T(8,128)} %get-tuple-element.24), channel_id=1, source_target_pairs={{0,128},{32,416},{64,192},{96,480},{128,256},{160,32},{192,320},{2... | collective-permute-start | bytes 786440 | tf_op jit(solution)/shard_map/ppermute | solution.py:181
  58.0 22.0 %collective-permute-start.1 = (f32[512,256]{1,0:T(8,128)S(1)}, f32[512,256]{1,0:T(8,128)S(1)}, u32[]{:S(2)}, u32[]{:S(2)}) collective-permute-start(f32[512,256]{1,0:T(8,128)S(1)} %get-tuple-element.21), channel_id=1, source_target_pairs={{0,64},{32,480},{64,128},{96,32},{128,192},{160,96},{192,256},{224... | collective-permute-start | bytes 1572872 | tf_op jit(solution)/shard_map/ppermute | solution.py:182
  65.7 18.6 %collective-permute-start.4 = (f32[512,256]{1,0:T(8,128)S(1)}, f32[512,256]{1,0:T(8,128)S(1)}, u32[]{:S(2)}, u32[]{:S(2)}) collective-permute-start(f32[512,256]{1,0:T(8,128)S(1)} %pad_maximum_fusion), channel_id=1, source_target_pairs={{0,128},{32,416},{64,192},{96,480},{128,256},{160,32},{192,320},{2... | collective-permute-start | bytes 1572872 | tf_op jit(solution)/shard_map/ppermute | solution.py:186
  70.1 27.8 %all-to-all-start.2 = ((f32[32,16,256]{2,1,0:T(8,128)}), f32[32,16,256]{2,1,0:T(8,128)S(1)}, u32[]{:S(2)}, u32[]{:S(2)}) async-start(f32[32,16,256]{2,1,0:T(8,128)} %broadcast_in_dim.5), calls=%async_computation.2 | async-start | bytes 1048576 | tf_op jit(solution)/shard_map/all_to_all | solution.py:190
  84.3 3.4 %collective-permute-start.5 = (f32[256,256]{1,0:T(8,128)S(1)}, f32[256,256]{1,0:T(8,128)S(1)}, u32[]{:S(2)}, u32[]{:S(2)}) collective-permute-start(f32[256,256]{1,0:T(8,128)S(1)} %slice_add_fusion.3), channel_id=1, source_target_pairs={{0,32},{32,0},{64,96},{96,64},{128,160},{160,128},{192,224},{224,1... | collective-permute-start | bytes 786440 | tf_op jit(solution)/shard_map/ppermute | solution.py:194

commit v4 on v3

v4 whole, which is shorter than its diff:
```python
import functools

import jax
import jax.numpy as jnp
from jax import lax
from jax.experimental import pallas as pl
from jax.experimental.pallas import tpu as pltpu
from jax.sharding import PartitionSpec as P

ROW_CONTRACT = (((1,), (1,)), ((), ()))
CODE_CONTRACT = (((0,), (0,)), ((), ()))
PLAIN = (((1,), (0,)), ((), ()))
VMEM = pl.BlockSpec(memory_space=pltpu.VMEM)
SMEM = pl.BlockSpec(memory_space=pltpu.SMEM)
HBM = pl.BlockSpec(memory_space=pltpu.HBM)
PARAMS = pltpu.CompilerParams(vmem_limit_bytes=24 * 1024 * 1024)


def dot(a, b, contract):
    return lax.dot_general(a, b, contract, preferred_element_type=jnp.float32)


def stats_kernel(tile, lat_hbm, up_hbm, book_hbm, out_ref, lat_ref, up_ref, book_ref, sems):
    parts = [pl.ds(start, tile) for start in range(0, book_hbm.shape[0], tile)]
    lat_load = pltpu.make_async_copy(lat_hbm, lat_ref, sems.at[len(parts)])
    up_load = pltpu.make_async_copy(up_hbm, up_ref, sems.at[len(parts) + 1])
    loads = [
        pltpu.make_async_copy(book_hbm.at[part], book_ref.at[part], sems.at[n])
        for n, part in enumerate(parts)
    ]
    for load in (lat_load, loads[0], up_load, *loads[1:]):
        load.start()
    lat_load.wait()
    tops, totals, weights = [], [], []
    for n, part in enumerate(parts):
        loads[n].wait()
        if n == 0:
            up_load.wait()
        book = book_ref[part, :]
        scores = dot(book, lat_ref[...], ROW_CONTRACT)
        dprob = dot(book, up_ref[...], ROW_CONTRACT)
        top = jnp.max(scores, axis=0, keepdims=True)
        expo = jnp.exp(scores - top)
        tops.append(top)
        totals.append(jnp.sum(expo, axis=0, keepdims=True))
        weights.append(jnp.sum(expo * dprob, axis=0, keepdims=True))
    top = functools.reduce(jnp.maximum, tops)
    shares = [jnp.exp(t - top) for t in tops]
    total = sum(s * t for s, t in zip(shares, totals))
    weight = sum(s * w for s, w in zip(shares, weights))
    stats = jnp.concatenate([top, total, weight], axis=0)
    out_ref[...] = jnp.broadcast_to(stats[None], out_ref.shape)


def chunk_ids(chips, y, core):
    step = 1 - 2 * core
    ids = []
    for far in range(1, chips // 2):
        chip = lax.rem(y + far * step + chips, chips)
        ids += [2 * chip + core, 2 * chip + 1 - core]
    return ids + [2 * lax.rem(y + chips // 2, chips) + core, 2 * y + core]


def half_step(chunk, start, row_ref, target_ref, lat_ref, up_ref, book_ref):
    lat, up = lat_ref[...], up_ref[...]
    book = book_ref[pl.ds(start, chunk), :]
    scores = dot(book, lat, ROW_CONTRACT)
    dprob = dot(book, up, ROW_CONTRACT)
    probs = jnp.exp(scores - row_ref[0:1, :]) * row_ref[1:2, :]
    soft = probs * (dprob + row_ref[2:3, :])
    codes = lax.broadcasted_iota(jnp.int32, soft.shape, 0)
    dscore = jnp.where(codes == target_ref[...] - start, soft - 1.0, soft).astype(jnp.bfloat16)
    return dscore, dot(dscore, lat, PLAIN) + dot(probs.astype(jnp.bfloat16), up, PLAIN)


def away_kernel(chunk, ids_ref, row_ref, target_ref, lat_ref, up_ref, book_ref, grad_ref, dscore_ref):
    half = grad_ref.shape[0] // chunk
    for n in range(half):
        start = pl.multiple_of(ids_ref[half + n] * chunk, chunk)
        here = slice(n * chunk, (n + 1) * chunk)
        dscore_ref[here, :], grad_ref[here, :] = half_step(
            chunk, start, row_ref, target_ref, lat_ref, up_ref, book_ref
        )


def mine_kernel(
    chunk, ids_ref, row_ref, target_ref, lat_ref, up_ref, book_ref, away_ref, grad_ref, out_ref
):
    total = jnp.zeros((book_ref.shape[1], lat_ref.shape[0]), jnp.float32)
    half = grad_ref.shape[0] // chunk
    for n in range(half):
        start = pl.multiple_of(ids_ref[n] * chunk, chunk)
        away_start = pl.multiple_of(ids_ref[half + n] * chunk, chunk)
        here = slice(n * chunk, (n + 1) * chunk)
        dscore, grad_ref[here, :] = half_step(
            chunk, start, row_ref, target_ref, lat_ref, up_ref, book_ref
        )
        total += dot(book_ref[pl.ds(start, chunk), :], dscore, CODE_CONTRACT)
        total += dot(book_ref[pl.ds(away_start, chunk), :], away_ref[here, :], CODE_CONTRACT)
    out_ref[...] = total.T


def merge_kernel(chunk, middle_ref, far_ref, across_ref, same_ref, cross_ref):
    same_ref[...] = middle_ref[:chunk, :] + far_ref[:chunk, :] + across_ref[...]
    cross_ref[...] = middle_ref[chunk:, :] + far_ref[chunk:, :]


def shards(latents, upstream, targets, codebook):
    rows, width = latents.shape
    local_codes = codebook.shape[0]
    n_code = lax.axis_size("code")
    n_dp = lax.axis_size("dp")
    chips = n_dp // 2
    chunk = local_codes // n_dp
    here = lax.axis_index("dp")
    y, core = here // 2, lax.rem(here, 2)
    macs = rows * local_codes * width
    f32, bf16 = jnp.float32, jnp.bfloat16

    tile = 1024
    stats = pl.pallas_call(
        functools.partial(stats_kernel, tile),
        out_shape=jax.ShapeDtypeStruct((n_code, 3, rows), f32),
        in_specs=[HBM] * 3,
        out_specs=VMEM,
        scratch_shapes=[
            pltpu.VMEM((rows, width), bf16),
            pltpu.VMEM((rows, width), bf16),
            pltpu.VMEM((local_codes, width), bf16),
            pltpu.SemaphoreType.DMA((local_codes // tile + 2,)),
        ],
        compiler_params=pltpu.CompilerParams(vmem_limit_bytes=60 * 1024 * 1024),
        cost_estimate=pl.CostEstimate(
            flops=4 * macs, bytes_accessed=3 << 20, transcendentals=rows * local_codes
        ),
        name="stats",
    )(latents, upstream, codebook)
    every = lax.all_to_all(stats, "code", 0, 0)
    tops = every[:, 0]
    top = jnp.max(tops, axis=0)
    share = jnp.exp(tops - top[None])
    total = jnp.sum(share * every[:, 1], axis=0)
    rowdot = jnp.sum(share * every[:, 2], axis=0) / total
    row = jnp.stack([top, 1.0 / total, 1.0 - rowdot])
    local_target = (targets - lax.axis_index("code") * local_codes)[None]

    ids = jnp.stack(chunk_ids(chips, y, core) + chunk_ids(chips, y, 1 - core))
    operands = (ids, row, local_target, latents, upstream, codebook)
    away, away_dscore = pl.pallas_call(
        functools.partial(away_kernel, chunk),
        out_shape=(
            jax.ShapeDtypeStruct((local_codes // 2, width), f32),
            jax.ShapeDtypeStruct((local_codes // 2, rows), bf16),
        ),
        in_specs=[SMEM] + [VMEM] * 5,
        out_specs=(VMEM, VMEM),
        compiler_params=PARAMS,
        cost_estimate=pl.CostEstimate(
            flops=4 * macs, bytes_accessed=6 << 20, transcendentals=rows * local_codes // 2
        ),
        name="away_half",
    )(*operands)
    got = lax.ppermute(away, "dp", [(i, i ^ 1) for i in range(n_dp)])
    half, lat_part = pl.pallas_call(
        functools.partial(mine_kernel, chunk),
        out_shape=(
            jax.ShapeDtypeStruct((local_codes // 2, width), f32),
            jax.ShapeDtypeStruct((rows, width), f32),
        ),
        in_specs=[SMEM] + [VMEM] * 6,
        out_specs=(VMEM, VMEM),
        compiler_params=PARAMS,
        cost_estimate=pl.CostEstimate(
            flops=6 * macs, bytes_accessed=7 << 20, transcendentals=rows * local_codes // 2
        ),
        name="mine_half",
    )(*operands, away_dscore)

    def along(far, other=0):
        return [
            (i, (i // 2 + far * (1 - 2 * (i % 2))) % chips * 2 + (i + other) % 2)
            for i in range(n_dp)
        ]

    *near, middle, far, across, own = [
        half[at : at + size] + got[at : at + size]
        for at, size in (
            (0, chunk),
            (chunk, chunk),
            (2 * chunk, 2 * chunk),
            (4 * chunk, 2 * chunk),
            (6 * chunk, chunk),
            (7 * chunk, chunk),
        )
    ]
    *near, middle, far, across, own, lat_part = lax.optimization_barrier(
        (*near, middle, far, across, own, lat_part)
    )
    far_came = lax.ppermute(far, "dp", along(1))
    across_came = lax.ppermute(across, "dp", along(2))
    near_came = [lax.ppermute(near[n], "dp", along(1, n)) for n in (0, 1)]
    merged = pl.pallas_call(
        functools.partial(merge_kernel, chunk),
        out_shape=[jax.ShapeDtypeStruct((chunk, width), f32)] * 2,
        in_specs=[VMEM] * 3,
        out_specs=[VMEM] * 2,
        compiler_params=PARAMS,
        cost_estimate=pl.CostEstimate(flops=6000000000, bytes_accessed=2 << 20, transcendentals=0),
        name="merge",
    )(middle, far_came, across_came)
    merged_came = [lax.ppermute(merged[n], "dp", along(2, n)) for n in (0, 1)]

    pieces = lax.all_to_all(lat_part.reshape(n_code, rows // n_code, width), "code", 0, 0)
    piece = jnp.sum(pieces, axis=0)
    latent_grad = lax.all_to_all(
        jnp.broadcast_to(piece[None], (n_code,) + piece.shape), "code", 0, 0
    ).reshape(rows, width)

    codebook_grad = near_came[0] + near_came[1] + merged_came[0] + merged_came[1] + own
    return (latent_grad, codebook_grad)


def solution(mesh):
    return jax.shard_map(
        shards,
        mesh=mesh,
        in_specs=(P("dp", None), P("dp", None), P("dp"), P("code", None)),
        out_specs=(P("dp", None), P(("code", "dp"), None)),
        check_vma=False,
    )
```

time: 99.3 us -> 95.8 us (0.965)
  the two profiles are of different devices: /device:TPU:72 before, /device:TPU:1 now
where the time goes in v4:
time: 95.8 us; the launch traced here: 95.2 us
  starting transfers between devices  55.7 us (58%)
  waiting for transfers between devices  20 us (21%)
  Pallas kernels  14.3 us (15%)
  other arithmetic  2.37 us (2%)
  local copies, waits for them, and re-layouts  1.76 us (2%)
  between operations  0.97 us (1%)
    all_to_all x1, starting transfers between devices, shards(): every = lax.all_to_all(stats, 'code', 0, 0)  13.7 us
    ppermute x2, waiting for transfers between devices, shards(): merged_came = [lax.ppermute(merged[n], 'dp', along(2, n)) for n in (0, 1)]  10.5 us
    all_to_all x1, starting transfers between devices, shards(): lax.all_to_all(jnp.broadcast_to(piece[None], (n_code,) + piece.shape), 'c...  9.5 us
    all_to_all x1, waiting for transfers between devices, shards(): every = lax.all_to_all(stats, 'code', 0, 0)  9.47 us
    ppermute x2, starting transfers between devices, shards(): merged_came = [lax.ppermute(merged[n], 'dp', along(2, n)) for n in (0, 1)]  7.8 us
    ppermute x2, starting transfers between devices, shards(): near_came = [lax.ppermute(near[n], 'dp', along(1, n)) for n in (0, 1)]  6.08 us
    pallas_call x1, Pallas kernels, shards(): pl.pallas_call(functools.partial(stats_kernel, tile), out_shape=jax.Shape...  5.83 us
    ppermute x1, starting transfers between devices, shards(): got = lax.ppermute(away, 'dp', [(i, i ^ 1) for i in range(n_dp)])  5.64 us
  transfers between devices with their start and end apart: 10, of which 3 were waited for; matrix products, arithmetic and copies ran while one was open for 3% of the time, Pallas kernels for 6%

profile of v4, /device:TPU:1, one launch (start us, length us, event | category | flops | bytes accessed | tf_op | source)
XLA Modules:
  0.0 95.2 jit_solution(12302424611209466904)
XLA Ops:
  0.6 0.0 copy-start
  0.6 0.0 copy-start.2
  0.7 0.0 copy-start.1
  0.7 0.0 copy-start.3
  0.7 5.8 %stats.1 = f32[32,3,512]{2,1,0:T(4,128)} custom-call(bf16[512,256]{1,0:T(8,128)(2,1)} %lat_ref.3, bf16[512,256]{1,0:T(8,128)(2,1)} %up_ref.3, bf16[4096,256]{1,0:T(8,128)(2,1)} %book_ref.3), custom_call_target="tpu_custom_call" | custom-call | flops 2147483648 | bytes 3145728 | tf_op jit(solution)/shard_map/stats/pallas_call | solution.py:121
  6.5 13.7 %all-to-all-start = ((f32[32,3,512]{2,1,0:T(4,128)}), f32[32,3,512]{2,1,0:T(4,128)S(1)}, u32[]{:S(2)}, u32[]{:S(2)}) async-start(f32[32,3,512]{2,1,0:T(4,128)} %stats.1), calls=%async_computation | async-start | bytes 524288 | tf_op jit(solution)/shard_map/all_to_all | solution.py:138
  20.3 0.1 stack.75.ids_ref
  20.4 0.0 copy-done.3
  20.5 9.5 %all-to-all-done = f32[32,3,512]{2,1,0:T(4,128)S(1)} async-done(((f32[32,3,512]{2,1,0:T(4,128)}), f32[32,3,512]{2,1,0:T(4,128)S(1)}, u32[]{:S(2)}, u32[]{:S(2)}) %all-to-all-start) | async-done | bytes 196640 | tf_op jit(solution)/shard_map/all_to_all | solution.py:138
  29.9 0.2 fusion.5
  30.2 0.0 copy-done
  30.2 0.0 copy-done.2
  30.2 0.0 copy-done.1
  30.2 3.0 %away_half.1 = (f32[2048,256]{1,0:T(8,128)S(1)}, bf16[2048,512]{1,0:T(8,128)(2,1)S(1)}) custom-call(s32[16]{0:T(128)S(1)} %stack.75.ids_ref, f32[3,512]{1,0:T(4,128)S(1)} %pad_maximum_fusion.row_ref, s32[1,512]{1,0:T(1,128)S(1)} %bitcast.42, bf16[512,256]{1,0:T(8,128)(2,1)S(1)} %copy-done.1, bf16[512,256]{1,0:T(8,128)(2,1)S(1)} %copy-done.2, ...), custom_call_target="tpu_custom_call" | custom-call | flops 2147483648 | bytes 6291456 | tf_op jit(solution)/shard_map/away_half/pallas_call | solution.py:149
  33.2 5.6 %collective-permute-start = (f32[2048,256]{1,0:T(8,128)S(1)}, f32[2048,256]{1,0:T(8,128)S(1)}, u32[]{:S(2)}, u32[]{:S(2)}) collective-permute-start(f32[2048,256]{1,0:T(8,128)S(1)} %get-tuple-element.17), channel_id=1, source_target_pairs={{0,32},{32,0},{64,96},{96,64},{128,160},{160,128},{192,224},{224,1... | collective-permute-start | bytes 6291464 | tf_op jit(solution)/shard_map/ppermute | solution.py:163
  38.9 5.4 %mine_half.1 = (f32[2048,256]{1,0:T(8,128)S(1)}, f32[512,256]{1,0:T(8,128)}) custom-call(s32[16]{0:T(128)S(1)} %stack.75.ids_ref, f32[3,512]{1,0:T(4,128)S(1)} %pad_maximum_fusion.row_ref, s32[1,512]{1,0:T(1,128)S(1)} %bitcast.43, bf16[512,256]{1,0:T(8,128)(2,1)S(1)} %copy-done.1, bf16[512,256]{1,0:T(8,128)(2,1)S(1)} %copy-done.2, ...), custom_call_target="tpu_custom_call" | custom-call | flops 3221225472 | bytes 7340032 | tf_op jit(solution)/shard_map/mine_half/pallas_call | solution.py:164
  44.3 0.0 collective-permute-done
  44.3 0.1 slice_add_fusion.2
  44.4 0.1 slice_add_fusion
  44.6 4.1 %all-to-all-start.1 = ((f32[32,16,256]{2,1,0:T(8,128)}), f32[32,16,256]{2,1,0:T(8,128)S(1)}, u32[]{:S(2)}, u32[]{:S(2)}) async-start(f32[32,16,256]{2,1,0:T(8,128)} %bitcast.22), calls=%async_computation.1 | async-start | bytes 1048576 | tf_op jit(solution)/shard_map/all_to_all | solution.py:213
  48.7 5.1 %collective-permute-start.3 = (f32[512,256]{1,0:T(8,128)S(1)}, f32[512,256]{1,0:T(8,128)S(1)}, u32[]{:S(2)}, u32[]{:S(2)}) collective-permute-start(f32[512,256]{1,0:T(8,128)S(1)} %get-tuple-element.23), channel_id=1, source_target_pairs={{0,64},{32,480},{64,128},{96,32},{128,192},{160,96},{192,256},{224... | collective-permute-start | bytes 1572872 | tf_op jit(solution)/shard_map/ppermute | solution.py:199
  53.8 3.8 %collective-permute-start.4 = (f32[256,256]{1,0:T(8,128)S(1)}, f32[256,256]{1,0:T(8,128)S(1)}, u32[]{:S(2)}, u32[]{:S(2)}) collective-permute-start(f32[256,256]{1,0:T(8,128)S(1)} %get-tuple-element.24), channel_id=1, source_target_pairs={{0,128},{32,416},{64,192},{96,480},{128,256},{160,32},{192,320},{2... | collective-permute-start | bytes 786440 | tf_op jit(solution)/shard_map/ppermute | solution.py:200
  57.6 3.0 %collective-permute-start.1 = (f32[256,256]{1,0:T(8,128)S(1)}, f32[256,256]{1,0:T(8,128)}, u32[]{:S(2)}, u32[]{:S(2)}) collective-permute-start(f32[256,256]{1,0:T(8,128)S(1)} %get-tuple-element.20), channel_id=1, source_target_pairs={{0,64},{32,480},{64,128},{96,32},{128,192},{160,96},{192,256},{224... | collective-permute-start | bytes 786440 | tf_op jit(solution)/shard_map/ppermute | solution.py:201
  60.6 3.1 %collective-permute-start.2 = (f32[256,256]{1,0:T(8,128)S(1)}, f32[256,256]{1,0:T(8,128)}, u32[]{:S(2)}, u32[]{:S(2)}) collective-permute-start(f32[256,256]{1,0:T(8,128)S(1)} %get-tuple-element.21), channel_id=1, source_target_pairs={{0,96},{32,448},{64,160},{96,0},{128,224},{160,64},{192,288},{224,... | collective-permute-start | bytes 786440 | tf_op jit(solution)/shard_map/ppermute | solution.py:201
  63.7 0.0 all-to-all-done.1
  63.8 0.9 broadcast_in_dim.5
  64.6 9.5 %all-to-all-start.2 = ((f32[32,16,256]{2,1,0:T(8,128)}), f32[32,16,256]{2,1,0:T(8,128)S(1)}, u32[]{:S(2)}, u32[]{:S(2)}) async-start(f32[32,16,256]{2,1,0:T(8,128)} %broadcast_in_dim.5), calls=%async_computation.2 | async-start | bytes 1048576 | tf_op jit(solution)/shard_map/all_to_all | solution.py:215
  74.1 0.0 collective-permute-done.4.across_ref
  74.1 0.0 collective-permute-done.3.far_ref
  74.1 0.1 merge.1
  74.2 3.6 %collective-permute-start.5 = (f32[256,256]{1,0:T(8,128)S(1)}, f32[256,256]{1,0:T(8,128)S(1)}, u32[]{:S(2)}, u32[]{:S(2)}) collective-permute-start(f32[256,256]{1,0:T(8,128)S(1)} %get-tuple-element.25), channel_id=1, source_target_pairs={{0,128},{32,416},{64,192},{96,480},{128,256},{160,32},{192,320},{2... | collective-permute-start | bytes 786440 | tf_op jit(solution)/shard_map/ppermute | solution.py:211
  77.9 4.2 %collective-permute-start.6 = (f32[256,256]{1,0:T(8,128)S(1)}, f32[256,256]{1,0:T(8,128)S(1)}, u32[]{:S(2)}, u32[]{:S(2)}) collective-permute-start(f32[256,256]{1,0:T(8,128)S(1)} %get-tuple-element.26), channel_id=1, source_target_pairs={{0,160},{32,384},{64,224},{96,448},{128,288},{160,0},{192,352},{22... | collective-permute-start | bytes 786440 | tf_op jit(solution)/shard_map/ppermute | solution.py:211
  82.0 0.0 collective-permute-done.1
  82.0 0.0 collective-permute-done.2
  82.0 4.6 %collective-permute-done.5 = f32[256,256]{1,0:T(8,128)S(1)} collective-permute-done((f32[256,256]{1,0:T(8,128)S(1)}, f32[256,256]{1,0:T(8,128)S(1)}, u32[]{:S(2)}, u32[]{:S(2)}) %collective-permute-start.5) | collective-permute-done | bytes 262176 | tf_op jit(solution)/shard_map/ppermute | solution.py:211
  86.6 5.9 %collective-permute-done.6 = f32[256,256]{1,0:T(8,128)S(1)} collective-permute-done((f32[256,256]{1,0:T(8,128)S(1)}, f32[256,256]{1,0:T(8,128)S(1)}, u32[]{:S(2)}, u32[]{:S(2)}) %collective-permute-start.6) | collective-permute-done | bytes 262176 | tf_op jit(solution)/shard_map/ppermute | solution.py:211
  92.6 1.8 %add_add_fusion = f32[256,256]{1,0:T(8,128)} fusion(f32[256,256]{1,0:T(8,128)S(1)} %get-tuple-element.27, f32[256,256]{1,0:T(8,128)S(1)} %collective-permute-done.6, f32[256,256]{1,0:T(8,128)S(1)} %collective-permute-done.5, f32[256,256]{1,0:T(8,128)} %collective-permute-done.1, f32[256,256]{1,0:T(8,128)} %collective-permute-done.2), kind=kLoop, calls=%fused_computation.6 | loop fusion | flops 262144 | bytes 1572864 | tf_op jit(solution)/shard_map/add | solution.py:219
  94.4 0.0 all-to-all-done.2
  94.4 0.8 copy.28
  (5 shorter events, 0.1 us)
Async XLA Ops:
  0.6 29.5 %copy-start = (bf16[4096,256]{1,0:T(8,128)(2,1)S(1)}, bf16[4096,256]{1,0:T(8,128)(2,1)}, u32[]{:S(2)}) copy-start(bf16[4096,256]{1,0:T(8,128)(2,1)} %book_ref.3) | copy-start | bytes 6291460
  0.6 29.5 %copy-start.2 = (bf16[512,256]{1,0:T(8,128)(2,1)S(1)}, bf16[512,256]{1,0:T(8,128)(2,1)}, u32[]{:S(2)}) copy-start(bf16[512,256]{1,0:T(8,128)(2,1)} %up_ref.3) | copy-start | bytes 786436
  0.7 29.5 %copy-start.1 = (bf16[512,256]{1,0:T(8,128)(2,1)S(1)}, bf16[512,256]{1,0:T(8,128)(2,1)}, u32[]{:S(2)}) copy-start(bf16[512,256]{1,0:T(8,128)(2,1)} %lat_ref.3) | copy-start | bytes 786436
  0.7 19.8 %copy-start.3 = (s32[512]{0:T(512)S(1)}, s32[512]{0:T(512)}, u32[]{:S(2)}) copy-start(s32[512]{0:T(512)} %param.6) | copy-start | bytes 6148
  6.5 23.4 %all-to-all-start = ((f32[32,3,512]{2,1,0:T(4,128)}), f32[32,3,512]{2,1,0:T(4,128)S(1)}, u32[]{:S(2)}, u32[]{:S(2)}) async-start(f32[32,3,512]{2,1,0:T(4,128)} %stats.1), calls=%async_computation | async-start | bytes 524288 | tf_op jit(solution)/shard_map/all_to_all | solution.py:138
  33.2 11.0 %collective-permute-start = (f32[2048,256]{1,0:T(8,128)S(1)}, f32[2048,256]{1,0:T(8,128)S(1)}, u32[]{:S(2)}, u32[]{:S(2)}) collective-permute-start(f32[2048,256]{1,0:T(8,128)S(1)} %get-tuple-element.17), channel_id=1, source_target_pairs={{0,32},{32,0},{64,96},{96,64},{128,160},{160,128},{192,224},{224,1... | collective-permute-start | bytes 6291464 | tf_op jit(solution)/shard_map/ppermute | solution.py:163
  44.6 19.1 %all-to-all-start.1 = ((f32[32,16,256]{2,1,0:T(8,128)}), f32[32,16,256]{2,1,0:T(8,128)S(1)}, u32[]{:S(2)}, u32[]{:S(2)}) async-start(f32[32,16,256]{2,1,0:T(8,128)} %bitcast.22), calls=%async_computation.1 | async-start | bytes 1048576 | tf_op jit(solution)/shard_map/all_to_all | solution.py:213
  48.7 25.4 %collective-permute-start.3 = (f32[512,256]{1,0:T(8,128)S(1)}, f32[512,256]{1,0:T(8,128)S(1)}, u32[]{:S(2)}, u32[]{:S(2)}) collective-permute-start(f32[512,256]{1,0:T(8,128)S(1)} %get-tuple-element.23), channel_id=1, source_target_pairs={{0,64},{32,480},{64,128},{96,32},{128,192},{160,96},{192,256},{224... | collective-permute-start | bytes 1572872 | tf_op jit(solution)/shard_map/ppermute | solution.py:199
  53.8 20.3 %collective-permute-start.4 = (f32[256,256]{1,0:T(8,128)S(1)}, f32[256,256]{1,0:T(8,128)S(1)}, u32[]{:S(2)}, u32[]{:S(2)}) collective-permute-start(f32[256,256]{1,0:T(8,128)S(1)} %get-tuple-element.24), channel_id=1, source_target_pairs={{0,128},{32,416},{64,192},{96,480},{128,256},{160,32},{192,320},{2... | collective-permute-start | bytes 786440 | tf_op jit(solution)/shard_map/ppermute | solution.py:200
  57.6 24.4 %collective-permute-start.1 = (f32[256,256]{1,0:T(8,128)S(1)}, f32[256,256]{1,0:T(8,128)}, u32[]{:S(2)}, u32[]{:S(2)}) collective-permute-start(f32[256,256]{1,0:T(8,128)S(1)} %get-tuple-element.20), channel_id=1, source_target_pairs={{0,64},{32,480},{64,128},{96,32},{128,192},{160,96},{192,256},{224... | collective-permute-start | bytes 786440 | tf_op jit(solution)/shard_map/ppermute | solution.py:201
  60.6 21.5 %collective-permute-start.2 = (f32[256,256]{1,0:T(8,128)S(1)}, f32[256,256]{1,0:T(8,128)}, u32[]{:S(2)}, u32[]{:S(2)}) collective-permute-start(f32[256,256]{1,0:T(8,128)S(1)} %get-tuple-element.21), channel_id=1, source_target_pairs={{0,96},{32,448},{64,160},{96,0},{128,224},{160,64},{192,288},{224,... | collective-permute-start | bytes 786440 | tf_op jit(solution)/shard_map/ppermute | solution.py:201
  64.6 29.8 %all-to-all-start.2 = ((f32[32,16,256]{2,1,0:T(8,128)}), f32[32,16,256]{2,1,0:T(8,128)S(1)}, u32[]{:S(2)}, u32[]{:S(2)}) async-start(f32[32,16,256]{2,1,0:T(8,128)} %broadcast_in_dim.5), calls=%async_computation.2 | async-start | bytes 1048576 | tf_op jit(solution)/shard_map/all_to_all | solution.py:215
  74.2 12.4 %collective-permute-start.5 = (f32[256,256]{1,0:T(8,128)S(1)}, f32[256,256]{1,0:T(8,128)S(1)}, u32[]{:S(2)}, u32[]{:S(2)}) collective-permute-start(f32[256,256]{1,0:T(8,128)S(1)} %get-tuple-element.25), channel_id=1, source_target_pairs={{0,128},{32,416},{64,192},{96,480},{128,256},{160,32},{192,320},{2... | collective-permute-start | bytes 786440 | tf_op jit(solution)/shard_map/ppermute | solution.py:211
  77.9 14.7 %collective-permute-start.6 = (f32[256,256]{1,0:T(8,128)S(1)}, f32[256,256]{1,0:T(8,128)S(1)}, u32[]{:S(2)}, u32[]{:S(2)}) collective-permute-start(f32[256,256]{1,0:T(8,128)S(1)} %get-tuple-element.26), channel_id=1, source_target_pairs={{0,160},{32,384},{64,224},{96,448},{128,288},{160,0},{192,352},{22... | collective-permute-start | bytes 786440 | tf_op jit(solution)/shard_map/ppermute | solution.py:211

commit v5 on v4

--- a/solution.py
+++ b/solution.py
@@ -54,11 +54,18 @@
 
 def chunk_ids(chips, y, core):
     step = 1 - 2 * core
-    ids = []
-    for far in range(1, chips // 2):
-        chip = lax.rem(y + far * step + chips, chips)
-        ids += [2 * chip + core, 2 * chip + 1 - core]
-    return ids + [2 * lax.rem(y + chips // 2, chips) + core, 2 * y + core]
+    near, middle, far = (2 * lax.rem(y + n * step + chips, chips) for n in (1, 2, 3))
+    across, same, other = 2 * lax.rem(y + chips // 2, chips), core, 1 - core
+    return [
+        near + same,
+        far + same,
+        far + other,
+        near + other,
+        middle + same,
+        middle + other,
+        across + same,
+        2 * y + same,
+    ]
 
 
 def half_step(chunk, start, row_ref, target_ref, lat_ref, up_ref, book_ref):
@@ -100,9 +107,13 @@
     out_ref[...] = total.T
 
 
-def merge_kernel(chunk, middle_ref, far_ref, across_ref, same_ref, cross_ref):
-    same_ref[...] = middle_ref[:chunk, :] + far_ref[:chunk, :] + across_ref[...]
-    cross_ref[...] = middle_ref[chunk:, :] + far_ref[chunk:, :]
+def merge_kernel(chunk, middle_ref, ahead_ref, across_ref, same_ref, cross_ref):
+    same_ref[...] = middle_ref[:chunk, :] + ahead_ref[chunk : 2 * chunk, :] + across_ref[...]
+    cross_ref[...] = middle_ref[chunk:, :] + ahead_ref[2 * chunk :, :]
+
+
+def hand_over_kernel(in_ref, out_ref):
+    out_ref[...] = in_ref[...]
 
 
 def shards(latents, upstream, targets, codebook):
@@ -182,32 +193,25 @@
             for i in range(n_dp)
         ]
 
-    *near, middle, far, across, own = [
-        half[at : at + size] + got[at : at + size]
-        for at, size in (
-            (0, chunk),
-            (chunk, chunk),
-            (2 * chunk, 2 * chunk),
-            (4 * chunk, 2 * chunk),
-            (6 * chunk, chunk),
-            (7 * chunk, chunk),
-        )
+    ahead, near_other, middle, across, own = [
+        half[at * chunk : to * chunk] + got[at * chunk : to * chunk]
+        for at, to in ((0, 3), (3, 4), (4, 6), (6, 7), (7, 8))
     ]
-    *near, middle, far, across, own, lat_part = lax.optimization_barrier(
-        (*near, middle, far, across, own, lat_part)
+    ahead, near_other, middle, across, own, lat_part = lax.optimization_barrier(
+        (ahead, near_other, middle, across, own, lat_part)
     )
-    far_came = lax.ppermute(far, "dp", along(1))
+    ahead_came = lax.ppermute(ahead, "dp", along(1))
     across_came = lax.ppermute(across, "dp", along(2))
-    near_came = [lax.ppermute(near[n], "dp", along(1, n)) for n in (0, 1)]
+    other_came = lax.ppermute(near_other, "dp", along(1, 1))
     merged = pl.pallas_call(
         functools.partial(merge_kernel, chunk),
         out_shape=[jax.ShapeDtypeStruct((chunk, width), f32)] * 2,
         in_specs=[VMEM] * 3,
         out_specs=[VMEM] * 2,
         compiler_params=PARAMS,
-        cost_estimate=pl.CostEstimate(flops=6000000000, bytes_accessed=2 << 20, transcendentals=0),
+        cost_estimate=pl.CostEstimate(flops=12000000000, bytes_accessed=2 << 20, transcendentals=0),
         name="merge",
-    )(middle, far_came, across_came)
+    )(middle, ahead_came, across_came)
     merged_came = [lax.ppermute(merged[n], "dp", along(2, n)) for n in (0, 1)]
 
     pieces = lax.all_to_all(lat_part.reshape(n_code, rows // n_code, width), "code", 0, 0)
@@ -216,7 +220,18 @@
         jnp.broadcast_to(piece[None], (n_code,) + piece.shape), "code", 0, 0
     ).reshape(rows, width)
 
-    codebook_grad = near_came[0] + near_came[1] + merged_came[0] + merged_came[1] + own
+    early = ahead_came[:chunk] + other_came + own
+    latent_grad = pl.pallas_call(
+        hand_over_kernel,
+        out_shape=pltpu.HBM((rows, width), f32),
+        in_specs=[VMEM],
+        out_specs=VMEM,
+        compiler_params=PARAMS,
+        cost_estimate=pl.CostEstimate(flops=0, bytes_accessed=1 << 20, transcendentals=0),
+        name="hand_over",
+    )(latent_grad)
+    latent_grad, early = lax.optimization_barrier((latent_grad, early))
+    codebook_grad = early + merged_came[0] + merged_came[1]
     return (latent_grad, codebook_grad)
 
 

time: 95.8 us -> 93.4 us (0.975)
  starting transfers between devices: 55.7 us -> 51.2 us
  waiting for transfers between devices: 20 us -> 22.2 us
    ppermute x2, waiting for transfers between devices: 10.5 us -> 4.36 us  [shards(): merged_came = [lax.ppermute(merged[n], 'dp', along(2, n)) for n in (0, 1)]]
    all_to_all x1, waiting for transfers between devices: 0.01 us -> 5 us  [shards(): lax.all_to_all(jnp.broadcast_to(piece[None], (n_code,) + piece.shape), 'c...]
    ppermute x3 -> x2, starting transfers between devices: 11.2 us -> 7.7 us  [the longest x1 5.11 us: shards(): ahead_came = lax.ppermute(ahead, 'dp', along(1))]
    all_to_all x1, waiting for transfers between devices: 0.01 us -> 3.38 us  [shards(): lax.all_to_all(lat_part.reshape(n_code, rows // n_code, width), 'code', 0...]
    all_to_all x1, starting transfers between devices: 9.5 us -> 7.37 us  [shards(): lax.all_to_all(jnp.broadcast_to(piece[None], (n_code,) + piece.shape), 'c...]
    ppermute x2, starting transfers between devices: 7.8 us -> 8.89 us  [shards(): merged_came = [lax.ppermute(merged[n], 'dp', along(2, n)) for n in (0, 1)]]
    add x3 -> x5, other arithmetic: 2.09 us -> 1.96 us  [the longest x3 1.16 us: shards(): half[at * chunk:to * chunk] + got[at * chunk:to * chunk]]
  transfers between devices with their start and end apart: 10 -> 9, of which waited for: 3 -> 4; matrix products, arithmetic and copies ran while one was open for 3% -> 1% of each run, Pallas kernels for 6% -> 7%
where the time goes in v5:
time: 93.4 us; the launch traced here: 92.8 us
  starting transfers between devices  51.2 us (55%)
  waiting for transfers between devices  22.2 us (24%)
  Pallas kernels  15.2 us (16%)
  other arithmetic  2.25 us (2%)
  local copies, waits for them, and re-layouts  0.96 us (1%)
  between operations  0.95 us (1%)
    all_to_all x1, starting transfers between devices, shards(): every = lax.all_to_all(stats, 'code', 0, 0)  13.7 us
    all_to_all x1, waiting for transfers between devices, shards(): every = lax.all_to_all(stats, 'code', 0, 0)  9.47 us
    ppermute x2, starting transfers between devices, shards(): merged_came = [lax.ppermute(merged[n], 'dp', along(2, n)) for n in (0, 1)]  8.89 us
    all_to_all x1, starting transfers between devices, shards(): lax.all_to_all(jnp.broadcast_to(piece[None], (n_code,) + piece.shape), 'c...  7.37 us
    pallas_call x1, Pallas kernels, shards(): pl.pallas_call(functools.partial(stats_kernel, tile), out_shape=jax.Shape...  5.83 us
    ppermute x1, starting transfers between devices, shards(): got = lax.ppermute(away, 'dp', [(i, i ^ 1) for i in range(n_dp)])  5.64 us
    pallas_call x1, Pallas kernels, shards(): pl.pallas_call(functools.partial(mine_kernel, chunk), out_shape=(jax.Shap...  5.4 us
    ppermute x1, starting transfers between devices, shards(): ahead_came = lax.ppermute(ahead, 'dp', along(1))  5.11 us
  transfers between devices with their start and end apart: 9, of which 4 were waited for; matrix products, arithmetic and copies ran while one was open for 1% of the time, Pallas kernels for 7%

profile of v5, /device:TPU:1, one launch (start us, length us, event | category | flops | bytes accessed | tf_op | source)
XLA Modules:
  0.0 92.8 jit_solution(2823180307525632149)
XLA Ops:
  0.6 0.0 copy-start
  0.6 0.0 copy-start.2
  0.7 0.0 copy-start.1
  0.7 0.0 copy-start.3
  0.7 5.8 %stats.1 = f32[32,3,512]{2,1,0:T(4,128)} custom-call(bf16[512,256]{1,0:T(8,128)(2,1)} %lat_ref.3, bf16[512,256]{1,0:T(8,128)(2,1)} %up_ref.3, bf16[4096,256]{1,0:T(8,128)(2,1)} %book_ref.3), custom_call_target="tpu_custom_call" | custom-call | flops 2147483648 | bytes 3145728 | tf_op jit(solution)/shard_map/stats/pallas_call | solution.py:132
  6.5 13.7 %all-to-all-start = ((f32[32,3,512]{2,1,0:T(4,128)}), f32[32,3,512]{2,1,0:T(4,128)S(1)}, u32[]{:S(2)}, u32[]{:S(2)}) async-start(f32[32,3,512]{2,1,0:T(4,128)} %stats.1), calls=%async_computation | async-start | bytes 524288 | tf_op jit(solution)/shard_map/all_to_all | solution.py:149
  20.3 0.1 stack.75.ids_ref
  20.4 0.0 copy-done.3
  20.5 9.5 %all-to-all-done = f32[32,3,512]{2,1,0:T(4,128)S(1)} async-done(((f32[32,3,512]{2,1,0:T(4,128)}), f32[32,3,512]{2,1,0:T(4,128)S(1)}, u32[]{:S(2)}, u32[]{:S(2)}) %all-to-all-start) | async-done | bytes 196640 | tf_op jit(solution)/shard_map/all_to_all | solution.py:149
  29.9 0.2 fusion.6
  30.2 0.0 copy-done
  30.2 0.0 copy-done.2
  30.2 0.0 copy-done.1
  30.2 3.0 %away_half.1 = (f32[2048,256]{1,0:T(8,128)S(1)}, bf16[2048,512]{1,0:T(8,128)(2,1)S(1)}) custom-call(s32[16]{0:T(128)S(1)} %stack.75.ids_ref, f32[3,512]{1,0:T(4,128)S(1)} %pad_maximum_fusion.row_ref, s32[1,512]{1,0:T(1,128)S(1)} %bitcast.43, bf16[512,256]{1,0:T(8,128)(2,1)S(1)} %copy-done.1, bf16[512,256]{1,0:T(8,128)(2,1)S(1)} %copy-done.2, ...), custom_call_target="tpu_custom_call" | custom-call | flops 2147483648 | bytes 6291456 | tf_op jit(solution)/shard_map/away_half/pallas_call | solution.py:160
  33.2 5.6 %collective-permute-start = (f32[2048,256]{1,0:T(8,128)S(1)}, f32[2048,256]{1,0:T(8,128)S(1)}, u32[]{:S(2)}, u32[]{:S(2)}) collective-permute-start(f32[2048,256]{1,0:T(8,128)S(1)} %get-tuple-element.18), channel_id=1, source_target_pairs={{0,32},{32,0},{64,96},{96,64},{128,160},{160,128},{192,224},{224,1... | collective-permute-start | bytes 6291464 | tf_op jit(solution)/shard_map/ppermute | solution.py:174
  38.9 5.4 %mine_half.1 = (f32[2048,256]{1,0:T(8,128)S(1)}, f32[512,256]{1,0:T(8,128)}) custom-call(s32[16]{0:T(128)S(1)} %stack.75.ids_ref, f32[3,512]{1,0:T(4,128)S(1)} %pad_maximum_fusion.row_ref, s32[1,512]{1,0:T(1,128)S(1)} %bitcast.44, bf16[512,256]{1,0:T(8,128)(2,1)S(1)} %copy-done.1, bf16[512,256]{1,0:T(8,128)(2,1)S(1)} %copy-done.2, ...), custom_call_target="tpu_custom_call" | custom-call | flops 3221225472 | bytes 7340032 | tf_op jit(solution)/shard_map/mine_half/pallas_call | solution.py:175
  44.3 0.0 collective-permute-done
  44.3 0.1 slice_add_fusion.1.middle_ref
  44.4 1.0 %slice_add_fusion = f32[768,256]{1,0:T(8,128)} fusion(f32[2048,256]{1,0:T(8,128)S(1)} %collective-permute-done, f32[2048,256]{1,0:T(8,128)S(1)} %get-tuple-element.17), kind=kLoop, calls=%fused_computation | loop fusion | flops 196608 | bytes 2359296 | tf_op jit(solution)/shard_map/add | solution.py:197
  45.4 0.1 slice_add_fusion.3
  45.5 4.1 %all-to-all-start.1 = ((f32[32,16,256]{2,1,0:T(8,128)}), f32[32,16,256]{2,1,0:T(8,128)S(1)}, u32[]{:S(2)}, u32[]{:S(2)}) async-start(f32[32,16,256]{2,1,0:T(8,128)} %bitcast.22), calls=%async_computation.1 | async-start | bytes 1048576 | tf_op jit(solution)/shard_map/all_to_all | solution.py:217
  49.6 5.1 %collective-permute-start.1 = (f32[768,256]{1,0:T(8,128)}, f32[768,256]{1,0:T(8,128)S(1)}, u32[]{:S(2)}, u32[]{:S(2)}) collective-permute-start(f32[768,256]{1,0:T(8,128)} %slice_add_fusion), channel_id=1, source_target_pairs={{0,64},{32,480},{64,128},{96,32},{128,192},{160,96},{192,256},{224... | collective-permute-start | bytes 2359304 | tf_op jit(solution)/shard_map/ppermute | solution.py:203
  54.7 3.8 %collective-permute-start.3 = (f32[256,256]{1,0:T(8,128)S(1)}, f32[256,256]{1,0:T(8,128)S(1)}, u32[]{:S(2)}, u32[]{:S(2)}) collective-permute-start(f32[256,256]{1,0:T(8,128)S(1)} %get-tuple-element.27), channel_id=1, source_target_pairs={{0,128},{32,416},{64,192},{96,480},{128,256},{160,32},{192,320},{2... | collective-permute-start | bytes 786440 | tf_op jit(solution)/shard_map/ppermute | solution.py:204
  58.5 2.6 %collective-permute-start.2 = (f32[256,256]{1,0:T(8,128)S(1)}, f32[256,256]{1,0:T(8,128)S(1)}, u32[]{:S(2)}, u32[]{:S(2)}) collective-permute-start(f32[256,256]{1,0:T(8,128)S(1)} %get-tuple-element.22), channel_id=1, source_target_pairs={{0,96},{32,448},{64,160},{96,0},{128,224},{160,64},{192,288},{224,... | collective-permute-start | bytes 786440 | tf_op jit(solution)/shard_map/ppermute | solution.py:205
  61.1 3.4 %all-to-all-done.1 = f32[32,16,256]{2,1,0:T(8,128)S(1)} async-done(((f32[32,16,256]{2,1,0:T(8,128)}), f32[32,16,256]{2,1,0:T(8,128)S(1)}, u32[]{:S(2)}, u32[]{:S(2)}) %all-to-all-start.1) | async-done | bytes 524320 | tf_op jit(solution)/shard_map/all_to_all | solution.py:217
  64.5 0.9 broadcast_in_dim.5
  65.4 7.4 %all-to-all-start.2 = ((f32[32,16,256]{2,1,0:T(8,128)}), f32[32,16,256]{2,1,0:T(8,128)S(1)}, u32[]{:S(2)}, u32[]{:S(2)}) async-start(f32[32,16,256]{2,1,0:T(8,128)} %broadcast_in_dim.5), calls=%async_computation.2 | async-start | bytes 1048576 | tf_op jit(solution)/shard_map/all_to_all | solution.py:219
  72.7 0.0 collective-permute-done.3.across_ref
  72.8 0.0 collective-permute-done.1.ahead_ref
  72.8 0.1 merge.1
  72.8 5.9 %collective-permute-start.4 = (f32[256,256]{1,0:T(8,128)S(1)}, f32[256,256]{1,0:T(8,128)S(1)}, u32[]{:S(2)}, u32[]{:S(2)}) collective-permute-start(f32[256,256]{1,0:T(8,128)S(1)} %get-tuple-element.28), channel_id=1, source_target_pairs={{0,128},{32,416},{64,192},{96,480},{128,256},{160,32},{192,320},{2... | collective-permute-start | bytes 786440 | tf_op jit(solution)/shard_map/ppermute | solution.py:215
  78.7 3.0 %collective-permute-start.5 = (f32[256,256]{1,0:T(8,128)S(1)}, f32[256,256]{1,0:T(8,128)S(1)}, u32[]{:S(2)}, u32[]{:S(2)}) collective-permute-start(f32[256,256]{1,0:T(8,128)S(1)} %get-tuple-element.29), channel_id=1, source_target_pairs={{0,160},{32,384},{64,224},{96,448},{128,288},{160,0},{192,352},{22... | collective-permute-start | bytes 786440 | tf_op jit(solution)/shard_map/ppermute | solution.py:215
  81.7 0.0 collective-permute-done.2
  81.8 0.1 fusion
  81.8 5.0 %all-to-all-done.2 = f32[32,16,256]{2,1,0:T(8,128)S(1)} async-done(((f32[32,16,256]{2,1,0:T(8,128)}), f32[32,16,256]{2,1,0:T(8,128)S(1)}, u32[]{:S(2)}, u32[]{:S(2)}) %all-to-all-start.2) | async-done | bytes 524320 | tf_op jit(solution)/shard_map/all_to_all | solution.py:219
  86.8 0.8 hand_over.1
  87.6 0.0 collective-permute-done.4
  87.6 4.4 %collective-permute-done.5 = f32[256,256]{1,0:T(8,128)S(1)} collective-permute-done((f32[256,256]{1,0:T(8,128)S(1)}, f32[256,256]{1,0:T(8,128)S(1)}, u32[]{:S(2)}, u32[]{:S(2)}) %collective-permute-start.5) | collective-permute-done | bytes 262176 | tf_op jit(solution)/shard_map/ppermute | solution.py:215
  92.0 0.8 add_add_fusion
  (5 shorter events, 0.1 us)
Async XLA Ops:
  0.6 29.5 %copy-start = (bf16[4096,256]{1,0:T(8,128)(2,1)S(1)}, bf16[4096,256]{1,0:T(8,128)(2,1)}, u32[]{:S(2)}) copy-start(bf16[4096,256]{1,0:T(8,128)(2,1)} %book_ref.3) | copy-start | bytes 6291460
  0.6 29.5 %copy-start.2 = (bf16[512,256]{1,0:T(8,128)(2,1)S(1)}, bf16[512,256]{1,0:T(8,128)(2,1)}, u32[]{:S(2)}) copy-start(bf16[512,256]{1,0:T(8,128)(2,1)} %up_ref.3) | copy-start | bytes 786436
  0.7 29.5 %copy-start.1 = (bf16[512,256]{1,0:T(8,128)(2,1)S(1)}, bf16[512,256]{1,0:T(8,128)(2,1)}, u32[]{:S(2)}) copy-start(bf16[512,256]{1,0:T(8,128)(2,1)} %lat_ref.3) | copy-start | bytes 786436
  0.7 19.8 %copy-start.3 = (s32[512]{0:T(512)S(1)}, s32[512]{0:T(512)}, u32[]{:S(2)}) copy-start(s32[512]{0:T(512)} %param.6) | copy-start | bytes 6148
  6.5 23.4 %all-to-all-start = ((f32[32,3,512]{2,1,0:T(4,128)}), f32[32,3,512]{2,1,0:T(4,128)S(1)}, u32[]{:S(2)}, u32[]{:S(2)}) async-start(f32[32,3,512]{2,1,0:T(4,128)} %stats.1), calls=%async_computation | async-start | bytes 524288 | tf_op jit(solution)/shard_map/all_to_all | solution.py:149
  33.2 11.0 %collective-permute-start = (f32[2048,256]{1,0:T(8,128)S(1)}, f32[2048,256]{1,0:T(8,128)S(1)}, u32[]{:S(2)}, u32[]{:S(2)}) collective-permute-start(f32[2048,256]{1,0:T(8,128)S(1)} %get-tuple-element.18), channel_id=1, source_target_pairs={{0,32},{32,0},{64,96},{96,64},{128,160},{160,128},{192,224},{224,1... | collective-permute-start | bytes 6291464 | tf_op jit(solution)/shard_map/ppermute | solution.py:174
  45.5 19.0 %all-to-all-start.1 = ((f32[32,16,256]{2,1,0:T(8,128)}), f32[32,16,256]{2,1,0:T(8,128)S(1)}, u32[]{:S(2)}, u32[]{:S(2)}) async-start(f32[32,16,256]{2,1,0:T(8,128)} %bitcast.22), calls=%async_computation.1 | async-start | bytes 1048576 | tf_op jit(solution)/shard_map/all_to_all | solution.py:217
  49.6 23.2 %collective-permute-start.1 = (f32[768,256]{1,0:T(8,128)}, f32[768,256]{1,0:T(8,128)S(1)}, u32[]{:S(2)}, u32[]{:S(2)}) collective-permute-start(f32[768,256]{1,0:T(8,128)} %slice_add_fusion), channel_id=1, source_target_pairs={{0,64},{32,480},{64,128},{96,32},{128,192},{160,96},{192,256},{224... | collective-permute-start | bytes 2359304 | tf_op jit(solution)/shard_map/ppermute | solution.py:203
  54.7 18.0 %collective-permute-start.3 = (f32[256,256]{1,0:T(8,128)S(1)}, f32[256,256]{1,0:T(8,128)S(1)}, u32[]{:S(2)}, u32[]{:S(2)}) collective-permute-start(f32[256,256]{1,0:T(8,128)S(1)} %get-tuple-element.27), channel_id=1, source_target_pairs={{0,128},{32,416},{64,192},{96,480},{128,256},{160,32},{192,320},{2... | collective-permute-start | bytes 786440 | tf_op jit(solution)/shard_map/ppermute | solution.py:204
  58.5 23.3 %collective-permute-start.2 = (f32[256,256]{1,0:T(8,128)S(1)}, f32[256,256]{1,0:T(8,128)S(1)}, u32[]{:S(2)}, u32[]{:S(2)}) collective-permute-start(f32[256,256]{1,0:T(8,128)S(1)} %get-tuple-element.22), channel_id=1, source_target_pairs={{0,96},{32,448},{64,160},{96,0},{128,224},{160,64},{192,288},{224,... | collective-permute-start | bytes 786440 | tf_op jit(solution)/shard_map/ppermute | solution.py:205
  65.4 21.5 %all-to-all-start.2 = ((f32[32,16,256]{2,1,0:T(8,128)}), f32[32,16,256]{2,1,0:T(8,128)S(1)}, u32[]{:S(2)}, u32[]{:S(2)}) async-start(f32[32,16,256]{2,1,0:T(8,128)} %broadcast_in_dim.5), calls=%async_computation.2 | async-start | bytes 1048576 | tf_op jit(solution)/shard_map/all_to_all | solution.py:219
  72.8 14.8 %collective-permute-start.4 = (f32[256,256]{1,0:T(8,128)S(1)}, f32[256,256]{1,0:T(8,128)S(1)}, u32[]{:S(2)}, u32[]{:S(2)}) collective-permute-start(f32[256,256]{1,0:T(8,128)S(1)} %get-tuple-element.28), channel_id=1, source_target_pairs={{0,128},{32,416},{64,192},{96,480},{128,256},{160,32},{192,320},{2... | collective-permute-start | bytes 786440 | tf_op jit(solution)/shard_map/ppermute | solution.py:215
  78.7 13.3 %collective-permute-start.5 = (f32[256,256]{1,0:T(8,128)S(1)}, f32[256,256]{1,0:T(8,128)S(1)}, u32[]{:S(2)}, u32[]{:S(2)}) collective-permute-start(f32[256,256]{1,0:T(8,128)S(1)} %get-tuple-element.29), channel_id=1, source_target_pairs={{0,160},{32,384},{64,224},{96,448},{128,288},{160,0},{192,352},{22... | collective-permute-start | bytes 786440 | tf_op jit(solution)/shard_map/ppermute | solution.py:215

commit v6 on v5

--- a/solution.py
+++ b/solution.py
@@ -20,8 +20,8 @@
     return lax.dot_general(a, b, contract, preferred_element_type=jnp.float32)
 
 
-def stats_kernel(tile, lat_hbm, up_hbm, book_hbm, out_ref, lat_ref, up_ref, book_ref, sems):
-    parts = [pl.ds(start, tile) for start in range(0, book_hbm.shape[0], tile)]
+def stats_kernel(edges, lat_hbm, up_hbm, book_hbm, out_ref, lat_ref, up_ref, book_ref, sems):
+    parts = [pl.ds(start, end - start) for start, end in zip(edges, edges[1:])]
     lat_load = pltpu.make_async_copy(lat_hbm, lat_ref, sems.at[len(parts)])
     up_load = pltpu.make_async_copy(up_hbm, up_ref, sems.at[len(parts) + 1])
     loads = [
@@ -34,10 +34,10 @@
     tops, totals, weights = [], [], []
     for n, part in enumerate(parts):
         loads[n].wait()
+        book = book_ref[part, :]
+        scores = dot(book, lat_ref[...], ROW_CONTRACT)
         if n == 0:
             up_load.wait()
-        book = book_ref[part, :]
-        scores = dot(book, lat_ref[...], ROW_CONTRACT)
         dprob = dot(book, up_ref[...], ROW_CONTRACT)
         top = jnp.max(scores, axis=0, keepdims=True)
         expo = jnp.exp(scores - top)
@@ -93,8 +93,8 @@
 def mine_kernel(
     chunk, ids_ref, row_ref, target_ref, lat_ref, up_ref, book_ref, away_ref, grad_ref, out_ref
 ):
-    total = jnp.zeros((book_ref.shape[1], lat_ref.shape[0]), jnp.float32)
     half = grad_ref.shape[0] // chunk
+    books, away_books, dscores = [], [], []
     for n in range(half):
         start = pl.multiple_of(ids_ref[n] * chunk, chunk)
         away_start = pl.multiple_of(ids_ref[half + n] * chunk, chunk)
@@ -102,8 +102,11 @@
         dscore, grad_ref[here, :] = half_step(
             chunk, start, row_ref, target_ref, lat_ref, up_ref, book_ref
         )
-        total += dot(book_ref[pl.ds(start, chunk), :], dscore, CODE_CONTRACT)
-        total += dot(book_ref[pl.ds(away_start, chunk), :], away_ref[here, :], CODE_CONTRACT)
+        books.append(book_ref[pl.ds(start, chunk), :])
+        away_books.append(book_ref[pl.ds(away_start, chunk), :])
+        dscores.append(dscore)
+    total = dot(jnp.concatenate(books), jnp.concatenate(dscores), CODE_CONTRACT)
+    total += dot(jnp.concatenate(away_books), away_ref[...], CODE_CONTRACT)
     out_ref[...] = total.T
 
 
@@ -128,9 +131,9 @@
     macs = rows * local_codes * width
     f32, bf16 = jnp.float32, jnp.bfloat16
 
-    tile = 1024
+    edges = (0, chunk, local_codes // 2, local_codes)
     stats = pl.pallas_call(
-        functools.partial(stats_kernel, tile),
+        functools.partial(stats_kernel, edges),
         out_shape=jax.ShapeDtypeStruct((n_code, 3, rows), f32),
         in_specs=[HBM] * 3,
         out_specs=VMEM,
@@ -138,7 +141,7 @@
             pltpu.VMEM((rows, width), bf16),
             pltpu.VMEM((rows, width), bf16),
             pltpu.VMEM((local_codes, width), bf16),
-            pltpu.SemaphoreType.DMA((local_codes // tile + 2,)),
+            pltpu.SemaphoreType.DMA((len(edges) + 1,)),
         ],
         compiler_params=pltpu.CompilerParams(vmem_limit_bytes=60 * 1024 * 1024),
         cost_estimate=pl.CostEstimate(

time: 93.4 us -> 92.9 us (level)
  transfers between devices with their start and end apart: 9 -> 9, of which waited for: 4 -> 4; matrix products, arithmetic and copies ran while one was open for 1% -> 1% of each run, Pallas kernels for 7% -> 6%
where the time goes in v6:
time: 92.9 us; the launch traced here: 92.2 us
  starting transfers between devices  51.2 us (55%)
  waiting for transfers between devices  22.2 us (24%)
  Pallas kernels  14.6 us (16%)
  other arithmetic  2.25 us (2%)
  local copies, waits for them, and re-layouts  0.96 us (1%)
  between operations  0.95 us (1%)
    all_to_all x1, starting transfers between devices, shards(): every = lax.all_to_all(stats, 'code', 0, 0)  13.7 us
    all_to_all x1, waiting for transfers between devices, shards(): every = lax.all_to_all(stats, 'code', 0, 0)  9.47 us
    ppermute x2, starting transfers between devices, shards(): merged_came = [lax.ppermute(merged[n], 'dp', along(2, n)) for n in (0, 1)]  8.88 us
    all_to_all x1, starting transfers between devices, shards(): lax.all_to_all(jnp.broadcast_to(piece[None], (n_code,) + piece.shape), 'c...  7.37 us
    pallas_call x1, Pallas kernels, shards(): pl.pallas_call(functools.partial(stats_kernel, edges), out_shape=jax.Shap...  5.72 us
    ppermute x1, starting transfers between devices, shards(): got = lax.ppermute(away, 'dp', [(i, i ^ 1) for i in range(n_dp)])  5.64 us
    ppermute x1, starting transfers between devices, shards(): ahead_came = lax.ppermute(ahead, 'dp', along(1))  5.1 us
    all_to_all x1, waiting for transfers between devices, shards(): lax.all_to_all(jnp.broadcast_to(piece[None], (n_code,) + piece.shape), 'c...  5.01 us
  transfers between devices with their start and end apart: 9, of which 4 were waited for; matrix products, arithmetic and copies ran while one was open for 1% of the time, Pallas kernels for 6%

profile of v6, /device:TPU:1, one launch (start us, length us, event | category | flops | bytes accessed | tf_op | source)
XLA Modules:
  0.0 92.2 jit_solution(14033969164254329872)
XLA Ops:
  0.6 0.0 copy-start
  0.6 0.0 copy-start.2
  0.7 0.0 copy-start.1
  0.7 0.0 copy-start.3
  0.7 5.7 %stats.1 = f32[32,3,512]{2,1,0:T(4,128)} custom-call(bf16[512,256]{1,0:T(8,128)(2,1)} %lat_ref.3, bf16[512,256]{1,0:T(8,128)(2,1)} %up_ref.3, bf16[4096,256]{1,0:T(8,128)(2,1)} %book_ref.3), custom_call_target="tpu_custom_call" | custom-call | flops 2147483648 | bytes 3145728 | tf_op jit(solution)/shard_map/stats/pallas_call | solution.py:135
  6.4 13.7 %all-to-all-start = ((f32[32,3,512]{2,1,0:T(4,128)}), f32[32,3,512]{2,1,0:T(4,128)S(1)}, u32[]{:S(2)}, u32[]{:S(2)}) async-start(f32[32,3,512]{2,1,0:T(4,128)} %stats.1), calls=%async_computation | async-start | bytes 524288 | tf_op jit(solution)/shard_map/all_to_all | solution.py:152
  20.2 0.1 stack.75.ids_ref
  20.3 0.0 copy-done.3
  20.3 9.5 %all-to-all-done = f32[32,3,512]{2,1,0:T(4,128)S(1)} async-done(((f32[32,3,512]{2,1,0:T(4,128)}), f32[32,3,512]{2,1,0:T(4,128)S(1)}, u32[]{:S(2)}, u32[]{:S(2)}) %all-to-all-start) | async-done | bytes 196640 | tf_op jit(solution)/shard_map/all_to_all | solution.py:152
  29.8 0.2 fusion.6
  30.1 0.0 copy-done
  30.1 0.0 copy-done.2
  30.1 0.0 copy-done.1
  30.1 3.0 %away_half.1 = (f32[2048,256]{1,0:T(8,128)S(1)}, bf16[2048,512]{1,0:T(8,128)(2,1)S(1)}) custom-call(s32[16]{0:T(128)S(1)} %stack.75.ids_ref, f32[3,512]{1,0:T(4,128)S(1)} %pad_maximum_fusion.row_ref, s32[1,512]{1,0:T(1,128)S(1)} %bitcast.43, bf16[512,256]{1,0:T(8,128)(2,1)S(1)} %copy-done.1, bf16[512,256]{1,0:T(8,128)(2,1)S(1)} %copy-done.2, ...), custom_call_target="tpu_custom_call" | custom-call | flops 2147483648 | bytes 6291456 | tf_op jit(solution)/shard_map/away_half/pallas_call | solution.py:163
  33.1 5.6 %collective-permute-start = (f32[2048,256]{1,0:T(8,128)S(1)}, f32[2048,256]{1,0:T(8,128)S(1)}, u32[]{:S(2)}, u32[]{:S(2)}) collective-permute-start(f32[2048,256]{1,0:T(8,128)S(1)} %get-tuple-element.18), channel_id=1, source_target_pairs={{0,32},{32,0},{64,96},{96,64},{128,160},{160,128},{192,224},{224,1... | collective-permute-start | bytes 6291464 | tf_op jit(solution)/shard_map/ppermute | solution.py:177
  38.8 5.0 %mine_half.1 = (f32[2048,256]{1,0:T(8,128)S(1)}, f32[512,256]{1,0:T(8,128)}) custom-call(s32[16]{0:T(128)S(1)} %stack.75.ids_ref, f32[3,512]{1,0:T(4,128)S(1)} %pad_maximum_fusion.row_ref, s32[1,512]{1,0:T(1,128)S(1)} %bitcast.44, bf16[512,256]{1,0:T(8,128)(2,1)S(1)} %copy-done.1, bf16[512,256]{1,0:T(8,128)(2,1)S(1)} %copy-done.2, ...), custom_call_target="tpu_custom_call" | custom-call | flops 3221225472 | bytes 7340032 | tf_op jit(solution)/shard_map/mine_half/pallas_call | solution.py:178
  43.8 0.0 collective-permute-done
  43.8 0.1 slice_add_fusion.1.middle_ref
  43.8 1.0 %slice_add_fusion = f32[768,256]{1,0:T(8,128)} fusion(f32[2048,256]{1,0:T(8,128)S(1)} %collective-permute-done, f32[2048,256]{1,0:T(8,128)S(1)} %get-tuple-element.17), kind=kLoop, calls=%fused_computation | loop fusion | flops 196608 | bytes 2359296 | tf_op jit(solution)/shard_map/add | solution.py:200
  44.8 0.1 slice_add_fusion.3
  44.9 4.1 %all-to-all-start.1 = ((f32[32,16,256]{2,1,0:T(8,128)}), f32[32,16,256]{2,1,0:T(8,128)S(1)}, u32[]{:S(2)}, u32[]{:S(2)}) async-start(f32[32,16,256]{2,1,0:T(8,128)} %bitcast.22), calls=%async_computation.1 | async-start | bytes 1048576 | tf_op jit(solution)/shard_map/all_to_all | solution.py:220
  49.1 5.1 %collective-permute-start.1 = (f32[768,256]{1,0:T(8,128)}, f32[768,256]{1,0:T(8,128)S(1)}, u32[]{:S(2)}, u32[]{:S(2)}) collective-permute-start(f32[768,256]{1,0:T(8,128)} %slice_add_fusion), channel_id=1, source_target_pairs={{0,64},{32,480},{64,128},{96,32},{128,192},{160,96},{192,256},{224... | collective-permute-start | bytes 2359304 | tf_op jit(solution)/shard_map/ppermute | solution.py:206
  54.2 3.8 %collective-permute-start.3 = (f32[256,256]{1,0:T(8,128)S(1)}, f32[256,256]{1,0:T(8,128)S(1)}, u32[]{:S(2)}, u32[]{:S(2)}) collective-permute-start(f32[256,256]{1,0:T(8,128)S(1)} %get-tuple-element.27), channel_id=1, source_target_pairs={{0,128},{32,416},{64,192},{96,480},{128,256},{160,32},{192,320},{2... | collective-permute-start | bytes 786440 | tf_op jit(solution)/shard_map/ppermute | solution.py:207
  57.9 2.6 %collective-permute-start.2 = (f32[256,256]{1,0:T(8,128)S(1)}, f32[256,256]{1,0:T(8,128)S(1)}, u32[]{:S(2)}, u32[]{:S(2)}) collective-permute-start(f32[256,256]{1,0:T(8,128)S(1)} %get-tuple-element.22), channel_id=1, source_target_pairs={{0,96},{32,448},{64,160},{96,0},{128,224},{160,64},{192,288},{224,... | collective-permute-start | bytes 786440 | tf_op jit(solution)/shard_map/ppermute | solution.py:208
  60.5 3.4 %all-to-all-done.1 = f32[32,16,256]{2,1,0:T(8,128)S(1)} async-done(((f32[32,16,256]{2,1,0:T(8,128)}), f32[32,16,256]{2,1,0:T(8,128)S(1)}, u32[]{:S(2)}, u32[]{:S(2)}) %all-to-all-start.1) | async-done | bytes 524320 | tf_op jit(solution)/shard_map/all_to_all | solution.py:220
  64.0 0.9 broadcast_in_dim.5
  64.8 7.4 %all-to-all-start.2 = ((f32[32,16,256]{2,1,0:T(8,128)}), f32[32,16,256]{2,1,0:T(8,128)S(1)}, u32[]{:S(2)}, u32[]{:S(2)}) async-start(f32[32,16,256]{2,1,0:T(8,128)} %broadcast_in_dim.5), calls=%async_computation.2 | async-start | bytes 1048576 | tf_op jit(solution)/shard_map/all_to_all | solution.py:222
  72.2 0.0 collective-permute-done.3.across_ref
  72.2 0.0 collective-permute-done.1.ahead_ref
  72.2 0.1 merge.1
  72.3 5.9 %collective-permute-start.4 = (f32[256,256]{1,0:T(8,128)S(1)}, f32[256,256]{1,0:T(8,128)S(1)}, u32[]{:S(2)}, u32[]{:S(2)}) collective-permute-start(f32[256,256]{1,0:T(8,128)S(1)} %get-tuple-element.28), channel_id=1, source_target_pairs={{0,128},{32,416},{64,192},{96,480},{128,256},{160,32},{192,320},{2... | collective-permute-start | bytes 786440 | tf_op jit(solution)/shard_map/ppermute | solution.py:218
  78.2 3.0 %collective-permute-start.5 = (f32[256,256]{1,0:T(8,128)S(1)}, f32[256,256]{1,0:T(8,128)S(1)}, u32[]{:S(2)}, u32[]{:S(2)}) collective-permute-start(f32[256,256]{1,0:T(8,128)S(1)} %get-tuple-element.29), channel_id=1, source_target_pairs={{0,160},{32,384},{64,224},{96,448},{128,288},{160,0},{192,352},{22... | collective-permute-start | bytes 786440 | tf_op jit(solution)/shard_map/ppermute | solution.py:218
  81.2 0.0 collective-permute-done.2
  81.2 0.1 fusion
  81.3 5.0 %all-to-all-done.2 = f32[32,16,256]{2,1,0:T(8,128)S(1)} async-done(((f32[32,16,256]{2,1,0:T(8,128)}), f32[32,16,256]{2,1,0:T(8,128)S(1)}, u32[]{:S(2)}, u32[]{:S(2)}) %all-to-all-start.2) | async-done | bytes 524320 | tf_op jit(solution)/shard_map/all_to_all | solution.py:222
  86.3 0.8 hand_over.1
  87.1 0.0 collective-permute-done.4
  87.1 4.4 %collective-permute-done.5 = f32[256,256]{1,0:T(8,128)S(1)} collective-permute-done((f32[256,256]{1,0:T(8,128)S(1)}, f32[256,256]{1,0:T(8,128)S(1)}, u32[]{:S(2)}, u32[]{:S(2)}) %collective-permute-start.5) | collective-permute-done | bytes 262176 | tf_op jit(solution)/shard_map/ppermute | solution.py:218
  91.5 0.8 add_add_fusion
  (5 shorter events, 0.1 us)
Async XLA Ops:
  0.6 29.4 %copy-start = (bf16[4096,256]{1,0:T(8,128)(2,1)S(1)}, bf16[4096,256]{1,0:T(8,128)(2,1)}, u32[]{:S(2)}) copy-start(bf16[4096,256]{1,0:T(8,128)(2,1)} %book_ref.3) | copy-start | bytes 6291460
  0.6 29.4 %copy-start.2 = (bf16[512,256]{1,0:T(8,128)(2,1)S(1)}, bf16[512,256]{1,0:T(8,128)(2,1)}, u32[]{:S(2)}) copy-start(bf16[512,256]{1,0:T(8,128)(2,1)} %up_ref.3) | copy-start | bytes 786436
  0.7 29.4 %copy-start.1 = (bf16[512,256]{1,0:T(8,128)(2,1)S(1)}, bf16[512,256]{1,0:T(8,128)(2,1)}, u32[]{:S(2)}) copy-start(bf16[512,256]{1,0:T(8,128)(2,1)} %lat_ref.3) | copy-start | bytes 786436
  0.7 19.7 %copy-start.3 = (s32[512]{0:T(512)S(1)}, s32[512]{0:T(512)}, u32[]{:S(2)}) copy-start(s32[512]{0:T(512)} %param.6) | copy-start | bytes 6148
  6.4 23.4 %all-to-all-start = ((f32[32,3,512]{2,1,0:T(4,128)}), f32[32,3,512]{2,1,0:T(4,128)S(1)}, u32[]{:S(2)}, u32[]{:S(2)}) async-start(f32[32,3,512]{2,1,0:T(4,128)} %stats.1), calls=%async_computation | async-start | bytes 524288 | tf_op jit(solution)/shard_map/all_to_all | solution.py:152
  33.1 10.6 %collective-permute-start = (f32[2048,256]{1,0:T(8,128)S(1)}, f32[2048,256]{1,0:T(8,128)S(1)}, u32[]{:S(2)}, u32[]{:S(2)}) collective-permute-start(f32[2048,256]{1,0:T(8,128)S(1)} %get-tuple-element.18), channel_id=1, source_target_pairs={{0,32},{32,0},{64,96},{96,64},{128,160},{160,128},{192,224},{224,1... | collective-permute-start | bytes 6291464 | tf_op jit(solution)/shard_map/ppermute | solution.py:177
  44.9 19.0 %all-to-all-start.1 = ((f32[32,16,256]{2,1,0:T(8,128)}), f32[32,16,256]{2,1,0:T(8,128)S(1)}, u32[]{:S(2)}, u32[]{:S(2)}) async-start(f32[32,16,256]{2,1,0:T(8,128)} %bitcast.22), calls=%async_computation.1 | async-start | bytes 1048576 | tf_op jit(solution)/shard_map/all_to_all | solution.py:220
  49.1 23.2 %collective-permute-start.1 = (f32[768,256]{1,0:T(8,128)}, f32[768,256]{1,0:T(8,128)S(1)}, u32[]{:S(2)}, u32[]{:S(2)}) collective-permute-start(f32[768,256]{1,0:T(8,128)} %slice_add_fusion), channel_id=1, source_target_pairs={{0,64},{32,480},{64,128},{96,32},{128,192},{160,96},{192,256},{224... | collective-permute-start | bytes 2359304 | tf_op jit(solution)/shard_map/ppermute | solution.py:206
  54.2 18.0 %collective-permute-start.3 = (f32[256,256]{1,0:T(8,128)S(1)}, f32[256,256]{1,0:T(8,128)S(1)}, u32[]{:S(2)}, u32[]{:S(2)}) collective-permute-start(f32[256,256]{1,0:T(8,128)S(1)} %get-tuple-element.27), channel_id=1, source_target_pairs={{0,128},{32,416},{64,192},{96,480},{128,256},{160,32},{192,320},{2... | collective-permute-start | bytes 786440 | tf_op jit(solution)/shard_map/ppermute | solution.py:207
  57.9 23.3 %collective-permute-start.2 = (f32[256,256]{1,0:T(8,128)S(1)}, f32[256,256]{1,0:T(8,128)S(1)}, u32[]{:S(2)}, u32[]{:S(2)}) collective-permute-start(f32[256,256]{1,0:T(8,128)S(1)} %get-tuple-element.22), channel_id=1, source_target_pairs={{0,96},{32,448},{64,160},{96,0},{128,224},{160,64},{192,288},{224,... | collective-permute-start | bytes 786440 | tf_op jit(solution)/shard_map/ppermute | solution.py:208
  64.8 21.5 %all-to-all-start.2 = ((f32[32,16,256]{2,1,0:T(8,128)}), f32[32,16,256]{2,1,0:T(8,128)S(1)}, u32[]{:S(2)}, u32[]{:S(2)}) async-start(f32[32,16,256]{2,1,0:T(8,128)} %broadcast_in_dim.5), calls=%async_computation.2 | async-start | bytes 1048576 | tf_op jit(solution)/shard_map/all_to_all | solution.py:222
  72.3 14.8 %collective-permute-start.4 = (f32[256,256]{1,0:T(8,128)S(1)}, f32[256,256]{1,0:T(8,128)S(1)}, u32[]{:S(2)}, u32[]{:S(2)}) collective-permute-start(f32[256,256]{1,0:T(8,128)S(1)} %get-tuple-element.28), channel_id=1, source_target_pairs={{0,128},{32,416},{64,192},{96,480},{128,256},{160,32},{192,320},{2... | collective-permute-start | bytes 786440 | tf_op jit(solution)/shard_map/ppermute | solution.py:218
  78.2 13.3 %collective-permute-start.5 = (f32[256,256]{1,0:T(8,128)S(1)}, f32[256,256]{1,0:T(8,128)S(1)}, u32[]{:S(2)}, u32[]{:S(2)}) collective-permute-start(f32[256,256]{1,0:T(8,128)S(1)} %get-tuple-element.29), channel_id=1, source_target_pairs={{0,160},{32,384},{64,224},{96,448},{128,288},{160,0},{192,352},{22... | collective-permute-start | bytes 786440 | tf_op jit(solution)/shard_map/ppermute | solution.py:218

commit v7 on v6

--- a/solution.py
+++ b/solution.py
@@ -132,17 +132,17 @@
     f32, bf16 = jnp.float32, jnp.bfloat16
 
     edges = (0, chunk, local_codes // 2, local_codes)
-    stats = pl.pallas_call(
+    stats, lat_held, up_held, book_held = pl.pallas_call(
         functools.partial(stats_kernel, edges),
-        out_shape=jax.ShapeDtypeStruct((n_code, 3, rows), f32),
-        in_specs=[HBM] * 3,
-        out_specs=VMEM,
-        scratch_shapes=[
+        out_shape=(
+            jax.ShapeDtypeStruct((n_code, 3, rows), f32),
             pltpu.VMEM((rows, width), bf16),
             pltpu.VMEM((rows, width), bf16),
             pltpu.VMEM((local_codes, width), bf16),
-            pltpu.SemaphoreType.DMA((len(edges) + 1,)),
-        ],
+        ),
+        in_specs=[HBM] * 3,
+        out_specs=(VMEM,) * 4,
+        scratch_shapes=[pltpu.SemaphoreType.DMA((len(edges) + 1,))],
         compiler_params=pltpu.CompilerParams(vmem_limit_bytes=60 * 1024 * 1024),
         cost_estimate=pl.CostEstimate(
             flops=4 * macs, bytes_accessed=3 << 20, transcendentals=rows * local_codes
@@ -159,7 +159,7 @@
     local_target = (targets - lax.axis_index("code") * local_codes)[None]
 
     ids = jnp.stack(chunk_ids(chips, y, core) + chunk_ids(chips, y, 1 - core))
-    operands = (ids, row, local_target, latents, upstream, codebook)
+    operands = (ids, row, local_target, lat_held, up_held, book_held)
     away, away_dscore = pl.pallas_call(
         functools.partial(away_kernel, chunk),
         out_shape=(

time: 92.9 us -> 92.6 us (level)
  no operation moved by 1% of the time
where the time goes in v7:
time: 92.6 us; the launch traced here: 92 us
  starting transfers between devices  51.2 us (55%)
  waiting for transfers between devices  22.2 us (24%)
  Pallas kernels  14.5 us (16%)
  other arithmetic  2.24 us (2%)
  local copies, waits for them, and re-layouts  0.95 us (1%)
    all_to_all x1, starting transfers between devices, shards(): every = lax.all_to_all(stats, 'code', 0, 0)  13.7 us
    all_to_all x1, waiting for transfers between devices, shards(): every = lax.all_to_all(stats, 'code', 0, 0)  9.47 us
    ppermute x2, starting transfers between devices, shards(): merged_came = [lax.ppermute(merged[n], 'dp', along(2, n)) for n in (0, 1)]  8.89 us
    all_to_all x1, starting transfers between devices, shards(): lax.all_to_all(jnp.broadcast_to(piece[None], (n_code,) + piece.shape), 'c...  7.37 us
    ppermute x1, starting transfers between devices, shards(): got = lax.ppermute(away, 'dp', [(i, i ^ 1) for i in range(n_dp)])  5.64 us
    pallas_call x1, Pallas kernels, shards(): pl.pallas_call(functools.partial(stats_kernel, edges), out_shape=(jax.Sha...  5.57 us
    ppermute x1, starting transfers between devices, shards(): ahead_came = lax.ppermute(ahead, 'dp', along(1))  5.1 us
    all_to_all x1, waiting for transfers between devices, shards(): lax.all_to_all(jnp.broadcast_to(piece[None], (n_code,) + piece.shape), 'c...  5.02 us
  transfers between devices with their start and end apart: 9, of which 4 were waited for; matrix products, arithmetic and copies ran while one was open for 1% of the time, Pallas kernels for 6%

profile of v7, /device:TPU:1, one launch (start us, length us, event | category | flops | bytes accessed | tf_op | source)
XLA Modules:
  0.0 92.0 jit_solution(8330484595959993181)
XLA Ops:
  0.6 0.0 copy-start
  0.6 5.6 %stats.1 = (f32[32,3,512]{2,1,0:T(4,128)}, bf16[512,256]{1,0:T(8,128)(2,1)S(1)}, bf16[512,256]{1,0:T(8,128)(2,1)S(1)}, bf16[4096,256]{1,0:T(8,128)(2,1)S(1)}) custom-call(bf16[512,256]{1,0:T(8,128)(2,1)} %lat_hbm.1, bf16[512,256]{1,0:T(8,128)(2,1)} %up_hbm.1, bf16[4096,256]{1,0:T(8,128)(2,1)} %book_hbm.1), custom_call_target="tpu_custom_call" | custom-call | flops 2147483648 | bytes 3145728 | tf_op jit(solution)/shard_map/stats/pallas_call | solution.py:135
  6.2 13.7 %all-to-all-start = ((f32[32,3,512]{2,1,0:T(4,128)}), f32[32,3,512]{2,1,0:T(4,128)S(1)}, u32[]{:S(2)}, u32[]{:S(2)}) async-start(f32[32,3,512]{2,1,0:T(4,128)} %get-tuple-element.20), calls=%async_computation | async-start | bytes 524288 | tf_op jit(solution)/shard_map/all_to_all | solution.py:152
  20.0 0.1 stack.75.ids_ref
  20.1 0.0 copy-done
  20.2 9.5 %all-to-all-done = f32[32,3,512]{2,1,0:T(4,128)S(1)} async-done(((f32[32,3,512]{2,1,0:T(4,128)}), f32[32,3,512]{2,1,0:T(4,128)S(1)}, u32[]{:S(2)}, u32[]{:S(2)}) %all-to-all-start) | async-done | bytes 196640 | tf_op jit(solution)/shard_map/all_to_all | solution.py:152
  29.6 0.2 fusion.6
  29.9 3.0 %away_half.1 = (f32[2048,256]{1,0:T(8,128)S(1)}, bf16[2048,512]{1,0:T(8,128)(2,1)S(1)}) custom-call(s32[16]{0:T(128)S(1)} %stack.75.ids_ref, f32[3,512]{1,0:T(4,128)S(1)} %pad_maximum_fusion.row_ref, s32[1,512]{1,0:T(1,128)S(1)} %bitcast.43, bf16[512,256]{1,0:T(8,128)(2,1)S(1)} %get-tuple-element.21.lat_ref, bf16[512,256]{1,0:T(8,128)(2,1)S(1)} %get-tuple-element.22.up_ref, ...), custom_call_target="tpu_custom_call" | custom-call | flops 2147483648 | bytes 6291456 | tf_op jit(solution)/shard_map/away_half/pallas_call | solution.py:163
  32.9 5.6 %collective-permute-start = (f32[2048,256]{1,0:T(8,128)S(1)}, f32[2048,256]{1,0:T(8,128)S(1)}, u32[]{:S(2)}, u32[]{:S(2)}) collective-permute-start(f32[2048,256]{1,0:T(8,128)S(1)} %get-tuple-element.26), channel_id=1, source_target_pairs={{0,32},{32,0},{64,96},{96,64},{128,160},{160,128},{192,224},{224,1... | collective-permute-start | bytes 6291464 | tf_op jit(solution)/shard_map/ppermute | solution.py:177
  38.6 5.0 %mine_half.1 = (f32[2048,256]{1,0:T(8,128)S(1)}, f32[512,256]{1,0:T(8,128)}) custom-call(s32[16]{0:T(128)S(1)} %stack.75.ids_ref, f32[3,512]{1,0:T(4,128)S(1)} %pad_maximum_fusion.row_ref, s32[1,512]{1,0:T(1,128)S(1)} %bitcast.44, bf16[512,256]{1,0:T(8,128)(2,1)S(1)} %get-tuple-element.21.lat_ref, bf16[512,256]{1,0:T(8,128)(2,1)S(1)} %get-tuple-element.22.up_ref, ...), custom_call_target="tpu_custom_call" | custom-call | flops 3221225472 | bytes 7340032 | tf_op jit(solution)/shard_map/mine_half/pallas_call | solution.py:178
  43.5 0.0 collective-permute-done
  43.6 0.1 slice_add_fusion.1.middle_ref
  43.6 1.0 %slice_add_fusion = f32[768,256]{1,0:T(8,128)} fusion(f32[2048,256]{1,0:T(8,128)S(1)} %collective-permute-done, f32[2048,256]{1,0:T(8,128)S(1)} %get-tuple-element.25), kind=kLoop, calls=%fused_computation | loop fusion | flops 196608 | bytes 2359296 | tf_op jit(solution)/shard_map/add | solution.py:200
  44.6 0.1 slice_add_fusion.3
  44.7 4.1 %all-to-all-start.1 = ((f32[32,16,256]{2,1,0:T(8,128)}), f32[32,16,256]{2,1,0:T(8,128)S(1)}, u32[]{:S(2)}, u32[]{:S(2)}) async-start(f32[32,16,256]{2,1,0:T(8,128)} %bitcast.22), calls=%async_computation.1 | async-start | bytes 1048576 | tf_op jit(solution)/shard_map/all_to_all | solution.py:220
  48.8 5.1 %collective-permute-start.1 = (f32[768,256]{1,0:T(8,128)}, f32[768,256]{1,0:T(8,128)S(1)}, u32[]{:S(2)}, u32[]{:S(2)}) collective-permute-start(f32[768,256]{1,0:T(8,128)} %slice_add_fusion), channel_id=1, source_target_pairs={{0,64},{32,480},{64,128},{96,32},{128,192},{160,96},{192,256},{224... | collective-permute-start | bytes 2359304 | tf_op jit(solution)/shard_map/ppermute | solution.py:206
  54.0 3.8 %collective-permute-start.3 = (f32[256,256]{1,0:T(8,128)S(1)}, f32[256,256]{1,0:T(8,128)S(1)}, u32[]{:S(2)}, u32[]{:S(2)}) collective-permute-start(f32[256,256]{1,0:T(8,128)S(1)} %get-tuple-element.35), channel_id=1, source_target_pairs={{0,128},{32,416},{64,192},{96,480},{128,256},{160,32},{192,320},{2... | collective-permute-start | bytes 786440 | tf_op jit(solution)/shard_map/ppermute | solution.py:207
  57.7 2.6 %collective-permute-start.2 = (f32[256,256]{1,0:T(8,128)S(1)}, f32[256,256]{1,0:T(8,128)S(1)}, u32[]{:S(2)}, u32[]{:S(2)}) collective-permute-start(f32[256,256]{1,0:T(8,128)S(1)} %get-tuple-element.30), channel_id=1, source_target_pairs={{0,96},{32,448},{64,160},{96,0},{128,224},{160,64},{192,288},{224,... | collective-permute-start | bytes 786440 | tf_op jit(solution)/shard_map/ppermute | solution.py:208
  60.3 3.4 %all-to-all-done.1 = f32[32,16,256]{2,1,0:T(8,128)S(1)} async-done(((f32[32,16,256]{2,1,0:T(8,128)}), f32[32,16,256]{2,1,0:T(8,128)S(1)}, u32[]{:S(2)}, u32[]{:S(2)}) %all-to-all-start.1) | async-done | bytes 524320 | tf_op jit(solution)/shard_map/all_to_all | solution.py:220
  63.7 0.9 broadcast_in_dim.5
  64.6 7.4 %all-to-all-start.2 = ((f32[32,16,256]{2,1,0:T(8,128)}), f32[32,16,256]{2,1,0:T(8,128)S(1)}, u32[]{:S(2)}, u32[]{:S(2)}) async-start(f32[32,16,256]{2,1,0:T(8,128)} %broadcast_in_dim.5), calls=%async_computation.2 | async-start | bytes 1048576 | tf_op jit(solution)/shard_map/all_to_all | solution.py:222
  72.0 0.0 collective-permute-done.3.across_ref
  72.0 0.0 collective-permute-done.1.ahead_ref
  72.0 0.1 merge.1
  72.1 5.9 %collective-permute-start.4 = (f32[256,256]{1,0:T(8,128)S(1)}, f32[256,256]{1,0:T(8,128)S(1)}, u32[]{:S(2)}, u32[]{:S(2)}) collective-permute-start(f32[256,256]{1,0:T(8,128)S(1)} %get-tuple-element.36), channel_id=1, source_target_pairs={{0,128},{32,416},{64,192},{96,480},{128,256},{160,32},{192,320},{2... | collective-permute-start | bytes 786440 | tf_op jit(solution)/shard_map/ppermute | solution.py:218
  78.0 3.0 %collective-permute-start.5 = (f32[256,256]{1,0:T(8,128)S(1)}, f32[256,256]{1,0:T(8,128)S(1)}, u32[]{:S(2)}, u32[]{:S(2)}) collective-permute-start(f32[256,256]{1,0:T(8,128)S(1)} %get-tuple-element.37), channel_id=1, source_target_pairs={{0,160},{32,384},{64,224},{96,448},{128,288},{160,0},{192,352},{22... | collective-permute-start | bytes 786440 | tf_op jit(solution)/shard_map/ppermute | solution.py:218
  81.0 0.0 collective-permute-done.2
  81.0 0.1 fusion
  81.0 5.0 %all-to-all-done.2 = f32[32,16,256]{2,1,0:T(8,128)S(1)} async-done(((f32[32,16,256]{2,1,0:T(8,128)}), f32[32,16,256]{2,1,0:T(8,128)S(1)}, u32[]{:S(2)}, u32[]{:S(2)}) %all-to-all-start.2) | async-done | bytes 524320 | tf_op jit(solution)/shard_map/all_to_all | solution.py:222
  86.1 0.8 hand_over.1
  86.9 0.0 collective-permute-done.4
  86.9 4.3 %collective-permute-done.5 = f32[256,256]{1,0:T(8,128)S(1)} collective-permute-done((f32[256,256]{1,0:T(8,128)S(1)}, f32[256,256]{1,0:T(8,128)S(1)}, u32[]{:S(2)}, u32[]{:S(2)}) %collective-permute-start.5) | collective-permute-done | bytes 262176 | tf_op jit(solution)/shard_map/ppermute | solution.py:218
  91.2 0.8 add_add_fusion
  (5 shorter events, 0.1 us)
Async XLA Ops:
  0.6 19.5 %copy-start = (s32[512]{0:T(512)S(1)}, s32[512]{0:T(512)}, u32[]{:S(2)}) copy-start(s32[512]{0:T(512)} %param.6) | copy-start | bytes 6148
  6.2 23.4 %all-to-all-start = ((f32[32,3,512]{2,1,0:T(4,128)}), f32[32,3,512]{2,1,0:T(4,128)S(1)}, u32[]{:S(2)}, u32[]{:S(2)}) async-start(f32[32,3,512]{2,1,0:T(4,128)} %get-tuple-element.20), calls=%async_computation | async-start | bytes 524288 | tf_op jit(solution)/shard_map/all_to_all | solution.py:152
  32.9 10.6 %collective-permute-start = (f32[2048,256]{1,0:T(8,128)S(1)}, f32[2048,256]{1,0:T(8,128)S(1)}, u32[]{:S(2)}, u32[]{:S(2)}) collective-permute-start(f32[2048,256]{1,0:T(8,128)S(1)} %get-tuple-element.26), channel_id=1, source_target_pairs={{0,32},{32,0},{64,96},{96,64},{128,160},{160,128},{192,224},{224,1... | collective-permute-start | bytes 6291464 | tf_op jit(solution)/shard_map/ppermute | solution.py:177
  44.7 19.0 %all-to-all-start.1 = ((f32[32,16,256]{2,1,0:T(8,128)}), f32[32,16,256]{2,1,0:T(8,128)S(1)}, u32[]{:S(2)}, u32[]{:S(2)}) async-start(f32[32,16,256]{2,1,0:T(8,128)} %bitcast.22), calls=%async_computation.1 | async-start | bytes 1048576 | tf_op jit(solution)/shard_map/all_to_all | solution.py:220
  48.8 23.2 %collective-permute-start.1 = (f32[768,256]{1,0:T(8,128)}, f32[768,256]{1,0:T(8,128)S(1)}, u32[]{:S(2)}, u32[]{:S(2)}) collective-permute-start(f32[768,256]{1,0:T(8,128)} %slice_add_fusion), channel_id=1, source_target_pairs={{0,64},{32,480},{64,128},{96,32},{128,192},{160,96},{192,256},{224... | collective-permute-start | bytes 2359304 | tf_op jit(solution)/shard_map/ppermute | solution.py:206
  54.0 18.0 %collective-permute-start.3 = (f32[256,256]{1,0:T(8,128)S(1)}, f32[256,256]{1,0:T(8,128)S(1)}, u32[]{:S(2)}, u32[]{:S(2)}) collective-permute-start(f32[256,256]{1,0:T(8,128)S(1)} %get-tuple-element.35), channel_id=1, source_target_pairs={{0,128},{32,416},{64,192},{96,480},{128,256},{160,32},{192,320},{2... | collective-permute-start | bytes 786440 | tf_op jit(solution)/shard_map/ppermute | solution.py:207
  57.7 23.3 %collective-permute-start.2 = (f32[256,256]{1,0:T(8,128)S(1)}, f32[256,256]{1,0:T(8,128)S(1)}, u32[]{:S(2)}, u32[]{:S(2)}) collective-permute-start(f32[256,256]{1,0:T(8,128)S(1)} %get-tuple-element.30), channel_id=1, source_target_pairs={{0,96},{32,448},{64,160},{96,0},{128,224},{160,64},{192,288},{224,... | collective-permute-start | bytes 786440 | tf_op jit(solution)/shard_map/ppermute | solution.py:208
  64.6 21.5 %all-to-all-start.2 = ((f32[32,16,256]{2,1,0:T(8,128)}), f32[32,16,256]{2,1,0:T(8,128)S(1)}, u32[]{:S(2)}, u32[]{:S(2)}) async-start(f32[32,16,256]{2,1,0:T(8,128)} %broadcast_in_dim.5), calls=%async_computation.2 | async-start | bytes 1048576 | tf_op jit(solution)/shard_map/all_to_all | solution.py:222
  72.1 14.8 %collective-permute-start.4 = (f32[256,256]{1,0:T(8,128)S(1)}, f32[256,256]{1,0:T(8,128)S(1)}, u32[]{:S(2)}, u32[]{:S(2)}) collective-permute-start(f32[256,256]{1,0:T(8,128)S(1)} %get-tuple-element.36), channel_id=1, source_target_pairs={{0,128},{32,416},{64,192},{96,480},{128,256},{160,32},{192,320},{2... | collective-permute-start | bytes 786440 | tf_op jit(solution)/shard_map/ppermute | solution.py:218
  78.0 13.3 %collective-permute-start.5 = (f32[256,256]{1,0:T(8,128)S(1)}, f32[256,256]{1,0:T(8,128)S(1)}, u32[]{:S(2)}, u32[]{:S(2)}) collective-permute-start(f32[256,256]{1,0:T(8,128)S(1)} %get-tuple-element.37), channel_id=1, source_target_pairs={{0,160},{32,384},{64,224},{96,448},{128,288},{160,0},{192,352},{22... | collective-permute-start | bytes 786440 | tf_op jit(solution)/shard_map/ppermute | solution.py:218

commit v8 on v7

--- a/solution.py
+++ b/solution.py
@@ -94,19 +94,19 @@
     chunk, ids_ref, row_ref, target_ref, lat_ref, up_ref, book_ref, away_ref, grad_ref, out_ref
 ):
     half = grad_ref.shape[0] // chunk
-    books, away_books, dscores = [], [], []
+    books, dscores = [], []
+    away_starts = [pl.multiple_of(ids_ref[half + n] * chunk, chunk) for n in range(half)]
+    away_books = [book_ref[pl.ds(start, chunk), :] for start in away_starts]
+    total = dot(jnp.concatenate(away_books), away_ref[...], CODE_CONTRACT)
     for n in range(half):
         start = pl.multiple_of(ids_ref[n] * chunk, chunk)
-        away_start = pl.multiple_of(ids_ref[half + n] * chunk, chunk)
         here = slice(n * chunk, (n + 1) * chunk)
         dscore, grad_ref[here, :] = half_step(
             chunk, start, row_ref, target_ref, lat_ref, up_ref, book_ref
         )
         books.append(book_ref[pl.ds(start, chunk), :])
-        away_books.append(book_ref[pl.ds(away_start, chunk), :])
         dscores.append(dscore)
-    total = dot(jnp.concatenate(books), jnp.concatenate(dscores), CODE_CONTRACT)
-    total += dot(jnp.concatenate(away_books), away_ref[...], CODE_CONTRACT)
+    total += dot(jnp.concatenate(books), jnp.concatenate(dscores), CODE_CONTRACT)
     out_ref[...] = total.T
 
 

time: 92.6 us -> 92.6 us (level)
  no operation moved by 1% of the time
where the time goes in v8:
time: 92.6 us; the launch traced here: 92 us
  starting transfers between devices  51.2 us (55%)
  waiting for transfers between devices  22.2 us (24%)
  Pallas kernels  14.5 us (16%)
  other arithmetic  2.24 us (2%)
  local copies, waits for them, and re-layouts  0.95 us (1%)
    all_to_all x1, starting transfers between devices, shards(): every = lax.all_to_all(stats, 'code', 0, 0)  13.7 us
    all_to_all x1, waiting for transfers between devices, shards(): every = lax.all_to_all(stats, 'code', 0, 0)  9.47 us
    ppermute x2, starting transfers between devices, shards(): merged_came = [lax.ppermute(merged[n], 'dp', along(2, n)) for n in (0, 1)]  8.89 us
    all_to_all x1, starting transfers between devices, shards(): lax.all_to_all(jnp.broadcast_to(piece[None], (n_code,) + piece.shape), 'c...  7.37 us
    ppermute x1, starting transfers between devices, shards(): got = lax.ppermute(away, 'dp', [(i, i ^ 1) for i in range(n_dp)])  5.64 us
    pallas_call x1, Pallas kernels, shards(): pl.pallas_call(functools.partial(stats_kernel, edges), out_shape=(jax.Sha...  5.57 us
    ppermute x1, starting transfers between devices, shards(): ahead_came = lax.ppermute(ahead, 'dp', along(1))  5.1 us
    all_to_all x1, waiting for transfers between devices, shards(): lax.all_to_all(jnp.broadcast_to(piece[None], (n_code,) + piece.shape), 'c...  5.02 us
  transfers between devices with their start and end apart: 9, of which 4 were waited for; matrix products, arithmetic and copies ran while one was open for 1% of the time, Pallas kernels for 6%

profile of v8, /device:TPU:1, one launch (start us, length us, event | category | flops | bytes accessed | tf_op | source)
XLA Modules:
  0.0 92.0 jit_solution(5247827832663553451)
XLA Ops:
  0.6 0.0 copy-start
  0.6 5.6 %stats.1 = (f32[32,3,512]{2,1,0:T(4,128)}, bf16[512,256]{1,0:T(8,128)(2,1)S(1)}, bf16[512,256]{1,0:T(8,128)(2,1)S(1)}, bf16[4096,256]{1,0:T(8,128)(2,1)S(1)}) custom-call(bf16[512,256]{1,0:T(8,128)(2,1)} %lat_hbm.1, bf16[512,256]{1,0:T(8,128)(2,1)} %up_hbm.1, bf16[4096,256]{1,0:T(8,128)(2,1)} %book_hbm.1), custom_call_target="tpu_custom_call" | custom-call | flops 2147483648 | bytes 3145728 | tf_op jit(solution)/shard_map/stats/pallas_call | solution.py:135
  6.2 13.7 %all-to-all-start = ((f32[32,3,512]{2,1,0:T(4,128)}), f32[32,3,512]{2,1,0:T(4,128)S(1)}, u32[]{:S(2)}, u32[]{:S(2)}) async-start(f32[32,3,512]{2,1,0:T(4,128)} %get-tuple-element.20), calls=%async_computation | async-start | bytes 524288 | tf_op jit(solution)/shard_map/all_to_all | solution.py:152
  20.0 0.1 stack.75.ids_ref
  20.1 0.0 copy-done
  20.2 9.5 %all-to-all-done = f32[32,3,512]{2,1,0:T(4,128)S(1)} async-done(((f32[32,3,512]{2,1,0:T(4,128)}), f32[32,3,512]{2,1,0:T(4,128)S(1)}, u32[]{:S(2)}, u32[]{:S(2)}) %all-to-all-start) | async-done | bytes 196640 | tf_op jit(solution)/shard_map/all_to_all | solution.py:152
  29.6 0.2 fusion.6
  29.9 3.0 %away_half.1 = (f32[2048,256]{1,0:T(8,128)S(1)}, bf16[2048,512]{1,0:T(8,128)(2,1)S(1)}) custom-call(s32[16]{0:T(128)S(1)} %stack.75.ids_ref, f32[3,512]{1,0:T(4,128)S(1)} %pad_maximum_fusion.row_ref, s32[1,512]{1,0:T(1,128)S(1)} %bitcast.43, bf16[512,256]{1,0:T(8,128)(2,1)S(1)} %get-tuple-element.21.lat_ref, bf16[512,256]{1,0:T(8,128)(2,1)S(1)} %get-tuple-element.22.up_ref, ...), custom_call_target="tpu_custom_call" | custom-call | flops 2147483648 | bytes 6291456 | tf_op jit(solution)/shard_map/away_half/pallas_call | solution.py:163
  32.9 5.6 %collective-permute-start = (f32[2048,256]{1,0:T(8,128)S(1)}, f32[2048,256]{1,0:T(8,128)S(1)}, u32[]{:S(2)}, u32[]{:S(2)}) collective-permute-start(f32[2048,256]{1,0:T(8,128)S(1)} %get-tuple-element.26), channel_id=1, source_target_pairs={{0,32},{32,0},{64,96},{96,64},{128,160},{160,128},{192,224},{224,1... | collective-permute-start | bytes 6291464 | tf_op jit(solution)/shard_map/ppermute | solution.py:177
  38.6 5.0 %mine_half.1 = (f32[2048,256]{1,0:T(8,128)S(1)}, f32[512,256]{1,0:T(8,128)}) custom-call(s32[16]{0:T(128)S(1)} %stack.75.ids_ref, f32[3,512]{1,0:T(4,128)S(1)} %pad_maximum_fusion.row_ref, s32[1,512]{1,0:T(1,128)S(1)} %bitcast.44, bf16[512,256]{1,0:T(8,128)(2,1)S(1)} %get-tuple-element.21.lat_ref, bf16[512,256]{1,0:T(8,128)(2,1)S(1)} %get-tuple-element.22.up_ref, ...), custom_call_target="tpu_custom_call" | custom-call | flops 3221225472 | bytes 7340032 | tf_op jit(solution)/shard_map/mine_half/pallas_call | solution.py:178
  43.5 0.0 collective-permute-done
  43.5 0.1 slice_add_fusion.1.middle_ref
  43.6 1.0 %slice_add_fusion = f32[768,256]{1,0:T(8,128)} fusion(f32[2048,256]{1,0:T(8,128)S(1)} %collective-permute-done, f32[2048,256]{1,0:T(8,128)S(1)} %get-tuple-element.25), kind=kLoop, calls=%fused_computation | loop fusion | flops 196608 | bytes 2359296 | tf_op jit(solution)/shard_map/add | solution.py:200
  44.6 0.1 slice_add_fusion.3
  44.7 4.1 %all-to-all-start.1 = ((f32[32,16,256]{2,1,0:T(8,128)}), f32[32,16,256]{2,1,0:T(8,128)S(1)}, u32[]{:S(2)}, u32[]{:S(2)}) async-start(f32[32,16,256]{2,1,0:T(8,128)} %bitcast.22), calls=%async_computation.1 | async-start | bytes 1048576 | tf_op jit(solution)/shard_map/all_to_all | solution.py:220
  48.8 5.1 %collective-permute-start.1 = (f32[768,256]{1,0:T(8,128)}, f32[768,256]{1,0:T(8,128)S(1)}, u32[]{:S(2)}, u32[]{:S(2)}) collective-permute-start(f32[768,256]{1,0:T(8,128)} %slice_add_fusion), channel_id=1, source_target_pairs={{0,64},{32,480},{64,128},{96,32},{128,192},{160,96},{192,256},{224... | collective-permute-start | bytes 2359304 | tf_op jit(solution)/shard_map/ppermute | solution.py:206
  53.9 3.8 %collective-permute-start.3 = (f32[256,256]{1,0:T(8,128)S(1)}, f32[256,256]{1,0:T(8,128)S(1)}, u32[]{:S(2)}, u32[]{:S(2)}) collective-permute-start(f32[256,256]{1,0:T(8,128)S(1)} %get-tuple-element.35), channel_id=1, source_target_pairs={{0,128},{32,416},{64,192},{96,480},{128,256},{160,32},{192,320},{2... | collective-permute-start | bytes 786440 | tf_op jit(solution)/shard_map/ppermute | solution.py:207
  57.7 2.6 %collective-permute-start.2 = (f32[256,256]{1,0:T(8,128)S(1)}, f32[256,256]{1,0:T(8,128)S(1)}, u32[]{:S(2)}, u32[]{:S(2)}) collective-permute-start(f32[256,256]{1,0:T(8,128)S(1)} %get-tuple-element.30), channel_id=1, source_target_pairs={{0,96},{32,448},{64,160},{96,0},{128,224},{160,64},{192,288},{224,... | collective-permute-start | bytes 786440 | tf_op jit(solution)/shard_map/ppermute | solution.py:208
  60.3 3.4 %all-to-all-done.1 = f32[32,16,256]{2,1,0:T(8,128)S(1)} async-done(((f32[32,16,256]{2,1,0:T(8,128)}), f32[32,16,256]{2,1,0:T(8,128)S(1)}, u32[]{:S(2)}, u32[]{:S(2)}) %all-to-all-start.1) | async-done | bytes 524320 | tf_op jit(solution)/shard_map/all_to_all | solution.py:220
  63.7 0.9 broadcast_in_dim.5
  64.6 7.4 %all-to-all-start.2 = ((f32[32,16,256]{2,1,0:T(8,128)}), f32[32,16,256]{2,1,0:T(8,128)S(1)}, u32[]{:S(2)}, u32[]{:S(2)}) async-start(f32[32,16,256]{2,1,0:T(8,128)} %broadcast_in_dim.5), calls=%async_computation.2 | async-start | bytes 1048576 | tf_op jit(solution)/shard_map/all_to_all | solution.py:222
  72.0 0.0 collective-permute-done.3.across_ref
  72.0 0.0 collective-permute-done.1.ahead_ref
  72.0 0.1 merge.1
  72.1 5.9 %collective-permute-start.4 = (f32[256,256]{1,0:T(8,128)S(1)}, f32[256,256]{1,0:T(8,128)S(1)}, u32[]{:S(2)}, u32[]{:S(2)}) collective-permute-start(f32[256,256]{1,0:T(8,128)S(1)} %get-tuple-element.36), channel_id=1, source_target_pairs={{0,128},{32,416},{64,192},{96,480},{128,256},{160,32},{192,320},{2... | collective-permute-start | bytes 786440 | tf_op jit(solution)/shard_map/ppermute | solution.py:218
  78.0 3.0 %collective-permute-start.5 = (f32[256,256]{1,0:T(8,128)S(1)}, f32[256,256]{1,0:T(8,128)S(1)}, u32[]{:S(2)}, u32[]{:S(2)}) collective-permute-start(f32[256,256]{1,0:T(8,128)S(1)} %get-tuple-element.37), channel_id=1, source_target_pairs={{0,160},{32,384},{64,224},{96,448},{128,288},{160,0},{192,352},{22... | collective-permute-start | bytes 786440 | tf_op jit(solution)/shard_map/ppermute | solution.py:218
  81.0 0.0 collective-permute-done.2
  81.0 0.1 fusion
  81.0 5.0 %all-to-all-done.2 = f32[32,16,256]{2,1,0:T(8,128)S(1)} async-done(((f32[32,16,256]{2,1,0:T(8,128)}), f32[32,16,256]{2,1,0:T(8,128)S(1)}, u32[]{:S(2)}, u32[]{:S(2)}) %all-to-all-start.2) | async-done | bytes 524320 | tf_op jit(solution)/shard_map/all_to_all | solution.py:222
  86.1 0.8 hand_over.1
  86.9 0.0 collective-permute-done.4
  86.9 4.3 %collective-permute-done.5 = f32[256,256]{1,0:T(8,128)S(1)} collective-permute-done((f32[256,256]{1,0:T(8,128)S(1)}, f32[256,256]{1,0:T(8,128)S(1)}, u32[]{:S(2)}, u32[]{:S(2)}) %collective-permute-start.5) | collective-permute-done | bytes 262176 | tf_op jit(solution)/shard_map/ppermute | solution.py:218
  91.2 0.8 add_add_fusion
  (5 shorter events, 0.1 us)
Async XLA Ops:
  0.6 19.5 %copy-start = (s32[512]{0:T(512)S(1)}, s32[512]{0:T(512)}, u32[]{:S(2)}) copy-start(s32[512]{0:T(512)} %param.6) | copy-start | bytes 6148
  6.2 23.4 %all-to-all-start = ((f32[32,3,512]{2,1,0:T(4,128)}), f32[32,3,512]{2,1,0:T(4,128)S(1)}, u32[]{:S(2)}, u32[]{:S(2)}) async-start(f32[32,3,512]{2,1,0:T(4,128)} %get-tuple-element.20), calls=%async_computation | async-start | bytes 524288 | tf_op jit(solution)/shard_map/all_to_all | solution.py:152
  32.9 10.6 %collective-permute-start = (f32[2048,256]{1,0:T(8,128)S(1)}, f32[2048,256]{1,0:T(8,128)S(1)}, u32[]{:S(2)}, u32[]{:S(2)}) collective-permute-start(f32[2048,256]{1,0:T(8,128)S(1)} %get-tuple-element.26), channel_id=1, source_target_pairs={{0,32},{32,0},{64,96},{96,64},{128,160},{160,128},{192,224},{224,1... | collective-permute-start | bytes 6291464 | tf_op jit(solution)/shard_map/ppermute | solution.py:177
  44.7 19.0 %all-to-all-start.1 = ((f32[32,16,256]{2,1,0:T(8,128)}), f32[32,16,256]{2,1,0:T(8,128)S(1)}, u32[]{:S(2)}, u32[]{:S(2)}) async-start(f32[32,16,256]{2,1,0:T(8,128)} %bitcast.22), calls=%async_computation.1 | async-start | bytes 1048576 | tf_op jit(solution)/shard_map/all_to_all | solution.py:220
  48.8 23.2 %collective-permute-start.1 = (f32[768,256]{1,0:T(8,128)}, f32[768,256]{1,0:T(8,128)S(1)}, u32[]{:S(2)}, u32[]{:S(2)}) collective-permute-start(f32[768,256]{1,0:T(8,128)} %slice_add_fusion), channel_id=1, source_target_pairs={{0,64},{32,480},{64,128},{96,32},{128,192},{160,96},{192,256},{224... | collective-permute-start | bytes 2359304 | tf_op jit(solution)/shard_map/ppermute | solution.py:206
  53.9 18.0 %collective-permute-start.3 = (f32[256,256]{1,0:T(8,128)S(1)}, f32[256,256]{1,0:T(8,128)S(1)}, u32[]{:S(2)}, u32[]{:S(2)}) collective-permute-start(f32[256,256]{1,0:T(8,128)S(1)} %get-tuple-element.35), channel_id=1, source_target_pairs={{0,128},{32,416},{64,192},{96,480},{128,256},{160,32},{192,320},{2... | collective-permute-start | bytes 786440 | tf_op jit(solution)/shard_map/ppermute | solution.py:207
  57.7 23.3 %collective-permute-start.2 = (f32[256,256]{1,0:T(8,128)S(1)}, f32[256,256]{1,0:T(8,128)S(1)}, u32[]{:S(2)}, u32[]{:S(2)}) collective-permute-start(f32[256,256]{1,0:T(8,128)S(1)} %get-tuple-element.30), channel_id=1, source_target_pairs={{0,96},{32,448},{64,160},{96,0},{128,224},{160,64},{192,288},{224,... | collective-permute-start | bytes 786440 | tf_op jit(solution)/shard_map/ppermute | solution.py:208
  64.6 21.5 %all-to-all-start.2 = ((f32[32,16,256]{2,1,0:T(8,128)}), f32[32,16,256]{2,1,0:T(8,128)S(1)}, u32[]{:S(2)}, u32[]{:S(2)}) async-start(f32[32,16,256]{2,1,0:T(8,128)} %broadcast_in_dim.5), calls=%async_computation.2 | async-start | bytes 1048576 | tf_op jit(solution)/shard_map/all_to_all | solution.py:222
  72.1 14.8 %collective-permute-start.4 = (f32[256,256]{1,0:T(8,128)S(1)}, f32[256,256]{1,0:T(8,128)S(1)}, u32[]{:S(2)}, u32[]{:S(2)}) collective-permute-start(f32[256,256]{1,0:T(8,128)S(1)} %get-tuple-element.36), channel_id=1, source_target_pairs={{0,128},{32,416},{64,192},{96,480},{128,256},{160,32},{192,320},{2... | collective-permute-start | bytes 786440 | tf_op jit(solution)/shard_map/ppermute | solution.py:218
  78.0 13.3 %collective-permute-start.5 = (f32[256,256]{1,0:T(8,128)S(1)}, f32[256,256]{1,0:T(8,128)S(1)}, u32[]{:S(2)}, u32[]{:S(2)}) collective-permute-start(f32[256,256]{1,0:T(8,128)S(1)} %get-tuple-element.37), channel_id=1, source_target_pairs={{0,160},{32,384},{64,224},{96,448},{128,288},{160,0},{192,352},{22... | collective-permute-start | bytes 786440 | tf_op jit(solution)/shard_map/ppermute | solution.py:218
